TPU v7x, 32 devices: a whole 2x2x4 slice. The times are simulated.
32 devices in a mesh: row: 16 (over z, x, core), col: 2 (over y).
Axes of the slice: x: 2, y: 2, z: 4, core: 2. Of those that a mesh axis runs over, the one named last changes fastest.
Arguments:
- a_blocks: bfloat16 [16, 2, 16, 128, 128], P('row', 'col'), may hold values from -6 to 6
- a_rows: int32 [16, 2, 16], P('row', 'col'), may hold values from 0 to 3
- b_blocks: bfloat16 [16, 2, 32, 128, 128], P('row', 'col'), may hold values from -0.25 to 0.25
- b_cols: int32 [16, 2, 32], P('row', 'col'), may hold values from 0 to 7
- pair_list: int32 [16, 2, 4, 2, 256], P('row', 'col'), may hold values from 0 to 31, as said below
- pair_count: int32 [16, 2, 4], P('row', 'col'), may hold values from 1 to 256, as said below
- row_order: int32 [16, 4], P('row'), may hold values from 0 to 3, each once within a row
Outputs:
- product_matrix: bfloat16 [8192, 2048], P('row', 'col')
Inputs may be any that keep to these rules, and one draw needn't show every extreme that they name: pair_list[..., 0, :] names a left slot below 16 and pair_list[..., 1, :] a right slot below 32; no list of one device and stop names the same pair twice. `pair_count`: in every stop some device's list is full.
All inputs are finite; a program needn't handle non-finite values.
Results may differ from a plain program's by a relative error of at most 0.001.
Values may be sent and summed in bfloat16 or wider, within the bound.
No kernel may reach another device: no remote copies, remote signals or barrier semaphores. Data moves between devices by JAX's collectives and lax.ppermute only.
A program may use at most 64 MiB of HBM per device.

v0:
```python
import functools

import jax
import jax.numpy as jnp
from jax import lax
from jax.experimental import pallas as pl
from jax.experimental.pallas import tpu as pltpu
from jax.sharding import PartitionSpec as P

CCOLS = 8
PARTS = 2
UNROLL = 16
HEAD = 16
VMEM_BYTES = 40 << 20
VMEM = pl.BlockSpec(memory_space=pltpu.VMEM)


def round_up(value, step):
    return value + -value % step


class Sizes:
    def __init__(self, n_stops, n_pairs, n_left, n_right, n_rows, n_col, edge):
        self.n_stops, self.n_pairs, self.n_rows, self.n_col = n_stops, n_pairs, n_rows, n_col
        self.n_left, self.n_right, self.edge = n_left, n_right, edge
        self.parts = PARTS
        self.per_part = n_right // PARTS
        self.zero_slot = n_col * n_left
        self.row_bits = (n_rows - 1).bit_length()
        self.key_bits = self.row_bits + (self.per_part - 1).bit_length()
        self.left_bits = self.zero_slot.bit_length()
        most = (n_pairs + self.per_part * n_rows) // 2
        self.width = round_up(round_up(most, UNROLL) + 1, 128)


def kernel_call(
    kernel,
    out_shape,
    operands,
    scalars=(),
    scratch=(),
    specs=None,
):
    return pl.pallas_call(
        kernel,
        out_shape=out_shape,
        grid_spec=pltpu.PrefetchScalarGridSpec(
            num_scalar_prefetch=len(scalars),
            in_specs=specs or [VMEM] * len(operands),
            out_specs=jax.tree.map(lambda _: VMEM, out_shape),
            scratch_shapes=list(scratch),
        ),
        compiler_params=pltpu.CompilerParams(vmem_limit_bytes=VMEM_BYTES),
        cost_estimate=pl.CostEstimate(flops=128, bytes_accessed=128, transcendentals=0),
    )(*scalars, *operands)


def pack_kernel(blocks_ref, ids_ref, *refs):
    part_refs, head_ref, sems = refs[:-2], refs[-2], refs[-1]
    rows = blocks_ref.shape[0] // len(part_refs)
    copies = [
        pltpu.make_async_copy(
            blocks_ref.at[pl.ds(part * rows, rows)], ref.at[pl.ds(HEAD, rows)], sems.at[part]
        )
        for part, ref in enumerate(part_refs)
    ]
    for copy in copies:
        copy.start()
    head_ref[...] = jnp.zeros_like(head_ref)
    head_ref[0:1, : ids_ref.shape[1]] = ids_ref[...].astype(jnp.float32)
    for ref in part_refs:
        ref[:HEAD, :] = head_ref[...].astype(ref.dtype)
    for copy in copies:
        copy.wait()


def pack(blocks, ids):
    edge = blocks.shape[-1]
    blocks = blocks.reshape(-1, edge)
    shape = (HEAD + blocks.shape[0] // PARTS, edge)
    return kernel_call(
        pack_kernel,
        [jax.ShapeDtypeStruct(shape, blocks.dtype)] * PARTS,
        [blocks, ids.reshape(1, -1)],
        scratch=[pltpu.VMEM((HEAD, edge), jnp.float32), pltpu.SemaphoreType.DMA((PARTS,))],
        specs=[pl.BlockSpec(memory_space=pl.ANY), VMEM],
    )


def ids_of(ref):
    return ref[:HEAD, :].astype(jnp.float32)[0:1, :]


def prepare_kernel(sizes, count_ref, order_ref, pairs_ref, *refs):
    id_refs, words_ref = refs[:-1], refs[-1]
    n_col, n_rows, parts = sizes.n_col, sizes.n_rows, sizes.parts
    n_pairs, width = sizes.n_pairs, sizes.width

    def total(mask, value, axis):
        return jnp.sum(jnp.where(mask, value, 0.0), axis=axis, keepdims=True)

    here = lax.axis_index("row")
    lane = lax.broadcasted_iota(jnp.int32, (n_pairs, 128), 1)
    slot = lax.broadcasted_iota(jnp.int32, (n_pairs, sizes.n_left), 1)
    down = lax.broadcasted_iota(jnp.int32, (n_pairs, 1), 0)
    across = lax.broadcasted_iota(jnp.int32, (1, n_pairs), 1)
    places = lax.broadcasted_iota(jnp.int32, (1, width), 1).astype(jnp.float32)
    dead = float(sizes.n_right * n_rows)
    lefts, keys = [], []
    key_matrix = jnp.zeros((n_pairs, 128), jnp.float32)
    for stop in range(sizes.n_stops):
        ahead = lax.rem(here + stop, n_col)
        ids = id_refs[0][...]
        for j in range(1, n_col):
            ids = jnp.where(ahead == j, id_refs[j][...], ids)
        left_row = jnp.zeros(ids.shape, jnp.float32)
        for i in range(n_rows):
            left_row = jnp.where(ids == i, order_ref[:, i : i + 1].astype(jnp.float32), left_row)
        left = pairs_ref[:, 2 * stop : 2 * stop + 1]
        right = pairs_ref[:, 2 * stop + 1 : 2 * stop + 2]
        key = right.astype(jnp.float32) * n_rows + total(slot == left, left_row, 1)
        key = jnp.where(down < count_ref[:, stop : stop + 1], key, dead)
        lefts.append((left + ahead * sizes.n_left - sizes.zero_slot).astype(jnp.float32))
        keys.append(key)
        key_matrix = jnp.where(lane == stop, key, key_matrix)
    key_rows = key_matrix.T
    cut = float(sizes.per_part * n_rows)

    def part_of(key):
        return sum(jnp.where(key >= part * cut, 1.0, 0.0) for part in range(1, parts))

    scale = [float(1 << sizes.key_bits), float(1 << (sizes.key_bits + sizes.left_bits))]
    empty = sizes.zero_slot * (scale[0] + scale[1])
    for stop in range(sizes.n_stops):
        left, key, other = lefts[stop], keys[stop], key_rows[stop : stop + 1, :]
        same = key == other
        rank = total(same & (across < down), 1.0, 1)
        other_rank = total(same & (down < across), 1.0, 0)
        other_opens = other_rank == 2.0 * jnp.floor(other_rank * 0.5)
        own_part, other_part = part_of(key), part_of(other)
        group = jnp.floor(rank * 0.5)
        opens = rank == 2.0 * group
        group += total((other < key) & (own_part == other_part) & other_opens, 1.0, 1)
        word = jnp.where(opens, left * scale[0] + key - own_part * cut, left * scale[1])
        for part in range(parts):
            counted = (own_part == float(part)) & (key < dead)
            words = empty + total(counted & (group == places), word, 0)
            words = jnp.where(places == width - 1.0, total(counted & opens, 1.0, 0), words)
            line = parts * stop + part
            words_ref[line : line + 1, :] = words.astype(jnp.int32)


def products_kernel(sizes, n_rights, layout, opens, closes, words_ref, *refs):
    n_sources = sizes.n_col if opens else 1
    sources, refs = refs[:n_sources], refs[n_sources:]
    right_refs, refs = refs[:n_rights], refs[n_rights:]
    start_ref = None
    if not opens:
        start_ref, refs = refs[0], refs[1:]
    out_ref, refs = refs[0], refs[1:]
    left_ref = sources[0]
    edge = sizes.edge
    if opens:
        left_ref, refs = refs[0], refs[1:]
        rows = sizes.n_left * edge
        for j, source in enumerate(sources):
            left_ref[j * rows : (j + 1) * rows, :] = source[...]
        left_ref[len(sources) * rows :, :] = jnp.zeros((edge, edge), left_ref.dtype)
    ids_ref, col_ref, copy_sem = refs[:3]
    total_ref = refs[3] if closes else out_ref
    for which, ref in enumerate(right_refs):
        ids_ref[which : which + 1, :] = ids_of(ref).astype(jnp.int32)
    copy = pltpu.make_async_copy(ids_ref, col_ref, copy_sem)
    copy.start()
    total_ref[...] = jnp.zeros_like(total_ref) if opens else start_ref[...]
    copy.wait()

    core, col = lax.rem(lax.axis_index("row"), 2), lax.axis_index("col")

    def block(ref, slot, head):
        return ref[pl.ds(pl.multiple_of(slot * edge + head, HEAD), edge), :]

    for array, head, part, ahead in layout:
        stop = jnp.where(
            core == 0,
            -1 if ahead[0] is None else ahead[0] - col,
            -1 if ahead[1] is None else ahead[1] - col,
        )
        used = (stop >= 0) & (stop < sizes.n_stops)
        line = jnp.clip(stop, 0, sizes.n_stops - 1) * sizes.parts + part
        count = jnp.where(used, words_ref[line, sizes.width - 1], 0)

        def groups(first, size, array=array, head=head, part=part, line=line):
            for member in range(size):
                word = words_ref[line, first + member]
                row = word & ((1 << sizes.row_bits) - 1)
                slot = (word & ((1 << sizes.key_bits) - 1)) >> sizes.row_bits
                word = word >> sizes.key_bits
                lefts = word & ((1 << sizes.left_bits) - 1), word >> sizes.left_bits
                target = row * CCOLS + col_ref[array, slot + part * sizes.per_part]
                right = block(right_refs[array], slot, head + HEAD)
                total_ref[target] += jnp.dot(
                    jnp.concatenate([block(left_ref, left, 0) for left in lefts], axis=1),
                    jnp.concatenate([right, right], axis=0),
                    preferred_element_type=jnp.float32,
                )

        steps = (count + UNROLL // 2 - 1) // UNROLL

        @pl.loop(0, steps)
        def _(step, groups=groups):
            groups(step * UNROLL, UNROLL)

        @pl.when(count > steps * UNROLL)
        def _(steps=steps, groups=groups):
            groups(steps * UNROLL, UNROLL // 2)

    if closes:
        for target in range(total_ref.shape[0]):
            row, col = divmod(target, CCOLS)
            out_ref[row * edge : (row + 1) * edge, col * edge : (col + 1) * edge] = total_ref[
                target
            ].astype(out_ref.dtype)


def per_device(a_blocks, a_rows, b_blocks, b_cols, pair_list, pair_count, row_order):
    n_row, n_col = lax.axis_size("row"), lax.axis_size("col")
    n_stops, n_pairs = pair_list.shape[2], pair_list.shape[4]
    sizes = Sizes(
        n_stops,
        n_pairs,
        a_blocks.shape[2],
        b_blocks.shape[2],
        row_order.shape[1],
        n_col,
        a_blocks.shape[3],
    )
    row = lax.axis_index("row")
    edge, sums = sizes.edge, (sizes.n_rows * CCOLS, sizes.edge, sizes.edge)
    reach = n_col + n_stops - 2
    chips = (reach + 1) // 2
    evens, odds = range(2, chips + 1, 2), range(1, chips + 1, 2)
    parts = range(PARTS)

    def from_ahead(block, axis, distance):
        size = lax.axis_size(axis)
        return lax.ppermute(block, axis, [((i + distance) % size, i) for i in range(size)])

    def swap(bit, lower, upper):
        mine = lower if lower is upper else jnp.where(row // bit % 2 == 1, upper, lower)
        return lax.ppermute(mine, "row", [(i ^ bit, i) for i in range(n_row)])

    def both(distance):
        return (distance, distance)

    def swapped(j):
        ahead = 2 * j + 1, 2 * j - 1
        return tuple(d if 1 <= d <= reach else None for d in ahead)

    left_ids = [a_rows.reshape(1, -1)]
    left_ids += [from_ahead(left_ids[0], "col", j) for j in range(1, n_col)]
    own = list(pack(b_blocks, b_cols))
    even = {j: [from_ahead(part, "row", 2 * j) for part in own] for j in range(2, chips + 2, 2)}
    left_own, left_ids = lax.optimization_barrier((a_blocks.reshape(-1, edge), left_ids))
    lefts = [left_own] + [from_ahead(left_own, "col", j) for j in range(1, n_col)]
    words = kernel_call(
        functools.partial(prepare_kernel, sizes),
        jax.ShapeDtypeStruct((PARTS * n_stops, sizes.width), jnp.int32),
        [pair_count.reshape(1, -1), row_order, pair_list.reshape(2 * n_stops, n_pairs).T]
        + left_ids,
    )

    def wait(part, *others):
        arrived, others = lax.optimization_barrier(([even[j][part] for j in even], others))
        for j, block in zip(even, arrived):
            even[j][part] = block
        return others

    def pass_on(part):
        sets = {0: own, **even}
        return {j: swap(2, sets[j + 1][part], sets[j - 1][part]) for j in odds}

    def add(total, pieces, closes=False):
        rights = list({id(piece[0]): piece[0] for piece in pieces}.values())
        places = {id(block): place for place, block in enumerate(rights)}
        layout = tuple((places[id(piece[0])], *piece[1:]) for piece in pieces)
        if closes:
            out_shape = jax.ShapeDtypeStruct((sizes.n_rows * edge, CCOLS * edge), jnp.bfloat16)
        else:
            out_shape = jax.ShapeDtypeStruct(sums, jnp.float32)
        if total is None:
            left_shape = ((sizes.zero_slot + 1) * edge, edge)
            out_shape = [out_shape, jax.ShapeDtypeStruct(left_shape, left_own.dtype)]
        lines = round_up(len(rights), 8)
        return kernel_call(
            functools.partial(
                products_kernel, sizes, len(rights), layout, total is None, closes
            ),
            out_shape,
            (lefts if total is None else [left_all])
            + rights
            + ([] if total is None else [total]),
            [words],
            [
                pltpu.VMEM((lines, 128), jnp.int32),
                pltpu.SMEM((lines, 128), jnp.int32),
                pltpu.SemaphoreType.DMA,
            ]
            + ([pltpu.VMEM(sums, jnp.float32)] if closes else []),
        )

    def pieces_of(j, part, block):
        pieces = [(block, 0, part, both(2 * j))]
        if j < chips:
            pieces.append((swap(1, block, block), 0, part, swapped(j)))
        return pieces

    def odd_pieces(part):
        return [piece for j in odds for piece in pieces_of(j, part, odd[part][j])]

    def even_pieces(part):
        return [piece for j in evens for piece in pieces_of(j, part, even[j][part])]

    def end_pieces(part):
        farthest = odd[part][chips] if chips % 2 else even[chips][part]
        ahead = swapped(0)[0], swapped(chips)[1]
        return [(swap(1, farthest, own[part]), 0, part, ahead)]

    def even_and_end(parts):
        pieces = []
        for part in parts:
            pieces += even_pieces(part) + ([] if chips % 2 else end_pieces(part))
        return pieces

    def odd_and_end(parts):
        pieces = []
        for part in parts:
            pieces += odd_pieces(part) + (end_pieces(part) if chips % 2 else [])
        return pieces

    odd = {}
    words, lefts = wait(0, words, lefts)
    odd[0] = pass_on(0)
    pieces = [(own[part], 0, part, both(0)) for part in parts]
    total, left_all = add(None, pieces + even_pieces(0))
    odd[0], total = wait(1, odd[0], total)
    odd[1] = pass_on(1)
    ends = [] if chips % 2 else end_pieces(0)
    total = add(total, odd_and_end((0,)) + ends + even_and_end((1,)))
    odd[1], total = lax.optimization_barrier((odd[1], total))
    return add(total, odd_and_end((1,)), closes=True)


def solution(mesh):
    placed = (
        P("row", "col", None, None, None),
        P("row", "col", None),
        P("row", "col", None, None, None),
        P("row", "col", None),
        P("row", "col", None, None, None),
        P("row", "col", None),
        P("row", None),
    )
    return jax.shard_map(
        per_device, mesh=mesh, in_specs=placed, out_specs=P("row", "col"), check_vma=False
    )
```

profile of v0, /device:TPU:0, one launch (start us, length us, event | category | flops | bytes accessed | tf_op | source)
XLA Modules:
  0.0 57.0 jit_solution(12239527427662786427)
XLA Ops:
  0.0 0.0 copy-start
  0.0 1.2 %copy-done = bf16[1,1,32,128,128]{4,3,2,1,0:T(8,128)(2,1)S(1)} copy-done((bf16[1,1,32,128,128]{4,3,2,1,0:T(8,128)(2,1)S(1)}, bf16[1,1,32,128,128]{4,3,2,1,0:T(8,128)(2,1)}, u32[]{:S(2)}) %copy-start) | copy-done | bytes 1048600
  1.2 0.0 copy-start.2
  1.2 0.7 %copy-done.2 = s32[1,1,32]{2,1,0:T(1,128)S(1)} copy-done((s32[1,1,32]{2,1,0:T(1,128)S(1)}, s32[1,1,32]{2,1,0:T(1,128)}, u32[]{:S(2)}) %copy-start.2) | copy-done | bytes 152
  1.9 0.0 copy-start.1
  1.9 0.1 shard_map.73
  2.0 5.1 %collective-permute-start = (bf16[2064,128]{1,0:T(8,128)(2,1)S(1)}, bf16[2064,128]{1,0:T(8,128)(2,1)S(1)}, u32[]{:S(2)}, u32[]{:S(2)}) collective-permute-start(bf16[2064,128]{1,0:T(8,128)(2,1)S(1)} %get-tuple-element.21.refs_2_), channel_id=1, source_target_pairs={{8,0},{10,2},{12,4},{14,6},{16,8},{18,10},{20,12},{22,14},{24,16},... | collective-permute-start | bytes 1585160 | tf_op jit(solution)/shard_map/ppermute | solution.py:247
  7.1 1.5 %collective-permute-start.1 = (s32[1,16]{1,0:T(1,128)}, s32[1,16]{1,0:T(1,128)S(1)}, u32[]{:S(2)}, u32[]{:S(2)}) collective-permute-start(s32[1,16]{1,0:T(1,128)} %bitcast.12), channel_id=1, source_target_pairs={{1,0},{0,1},{3,2},{2,3},{5,4},{4,5},{7,6},{6,7},{9,8},{8,9},{11,10... | collective-permute-start | bytes 200 | tf_op jit(solution)/shard_map/ppermute | solution.py:247
  8.6 2.2 %collective-permute-done.1.refs_1_ = s32[1,16]{1,0:T(1,128)S(1)} collective-permute-done((s32[1,16]{1,0:T(1,128)}, s32[1,16]{1,0:T(1,128)S(1)}, u32[]{:S(2)}, u32[]{:S(2)}) %collective-permute-start.1) | collective-permute-done | bytes 96 | tf_op jit(solution)/shard_map/ppermute | solution.py:247
  10.8 1.5 %collective-permute-start.2 = (bf16[2048,128]{1,0:T(8,128)(2,1)}, bf16[2048,128]{1,0:T(8,128)(2,1)S(1)}, u32[]{:S(2)}, u32[]{:S(2)}) collective-permute-start(bf16[2048,128]{1,0:T(8,128)(2,1)} %bitcast.7), channel_id=1, source_target_pairs={{1,0},{0,1},{3,2},{2,3},{5,4},{4,5},{7,6},{6,7},{9,8},{8,9},{11,10... | collective-permute-start | bytes 1572872 | tf_op jit(solution)/shard_map/ppermute | solution.py:247
  12.3 0.4 collective-permute-start.3
  12.7 0.7 %reshape.21 = s32[8,256]{1,0:T(8,128)S(1)} reshape(s32[1,1,4,2,256]{4,3,2,1,0:T(2,128)} %param.11) | data formatting | bytes 16384 | tf_op jit(solution)/shard_map/reshape | solution.py:269
  13.4 0.1 copy.9
  13.6 0.0 copy-start.3
  13.6 0.7 %copy-done.3 = s32[1,1,4]{2,1,0:T(1,128)S(1)} copy-done((s32[1,1,4]{2,1,0:T(1,128)S(1)}, s32[1,1,4]{2,1,0:T(1,128)}, u32[]{:S(2)}) %copy-start.3) | copy-done | bytes 40
  14.2 0.0 copy-start.4
  14.2 0.7 %copy-done.4 = s32[1,4]{1,0:T(1,128)S(1)} copy-done((s32[1,4]{1,0:T(1,128)S(1)}, s32[1,4]{1,0:T(1,128)}, u32[]{:S(2)}) %copy-start.4) | copy-done | bytes 40
  14.9 0.0 copy-start.5
  14.9 0.7 %copy-done.5 = s32[1,1,16]{2,1,0:T(1,128)S(1)} copy-done((s32[1,1,16]{2,1,0:T(1,128)S(1)}, s32[1,1,16]{2,1,0:T(1,128)}, u32[]{:S(2)}) %copy-start.5) | copy-done | bytes 88
  15.6 2.9 %shard_map.74.words_ref = s32[8,256]{1,0:T(8,128)S(1)} custom-call(s32[1,4]{1,0:T(1,128)S(1)} %bitcast.11, s32[1,4]{1,0:T(1,128)S(1)} %copy-done.4, s32[256,8]{1,0:T(8,128)S(1)} %bitcast.9, s32[1,16]{1,0:T(1,128)S(1)} %bitcast.13, s32[1,16]{1,0:T(1,128)S(1)} %collective-permute-done.1.refs_1_), custom_call_target="tpu_custom_call" | custom-call | flops 128 | bytes 128 | tf_op jit(solution)/shard_map/pallas_call | solution.py:44
  18.4 5.1 %collective-permute-done.2.refs_1_ = bf16[2048,128]{1,0:T(8,128)(2,1)S(1)} collective-permute-done((bf16[2048,128]{1,0:T(8,128)(2,1)}, bf16[2048,128]{1,0:T(8,128)(2,1)S(1)}, u32[]{:S(2)}, u32[]{:S(2)}) %collective-permute-start.2) | collective-permute-done | bytes 524320 | tf_op jit(solution)/shard_map/ppermute | solution.py:247
  23.5 0.0 collective-permute-done.refs_4_
  23.5 0.1 broadcast_select_fusion.1
  23.6 1.6 %collective-permute-start.4 = (bf16[2064,128]{1,0:T(8,128)(2,1)S(1)}, bf16[2064,128]{1,0:T(8,128)(2,1)S(1)}, u32[]{:S(2)}, u32[]{:S(2)}) collective-permute-start(bf16[2064,128]{1,0:T(8,128)(2,1)S(1)} %get-tuple-element.40), channel_id=1, source_target_pairs={{4,0},{6,2},{0,4},{2,6},{12,8},{14,10},{8,12},{10,14},{20,16},{22,... | collective-permute-start | bytes 1585160 | tf_op jit(solution)/shard_map/ppermute | solution.py:251
  25.2 0.0 collective-permute-start.7
  25.2 0.0 copy-done.1
  25.2 1.8 %shard_map.75 = (f32[32,128,128]{2,1,0:T(8,128)S(1)}, bf16[4224,128]{1,0:T(8,128)(2,1)S(1)}) custom-call(s32[8,256]{1,0:T(8,128)S(1)} %shard_map.74.words_ref, bf16[2048,128]{1,0:T(8,128)(2,1)S(1)} %bitcast.8, bf16[2048,128]{1,0:T(8,128)(2,1)S(1)} %collective-permute-done.2.refs_1_, bf16[2064,128]{1,0:T(8,128)(2,1)S(1)} %get-tuple-element.21.refs_2_, ...), custom_call_target="tpu_custom_call" | custom-call | flops 128 | bytes 128 | tf_op jit(solution)/shard_map/pallas_call | solution.py:44
  27.0 2.7 %collective-permute-done.3.refs_4_ = bf16[2064,128]{1,0:T(8,128)(2,1)S(1)} collective-permute-done((bf16[2064,128]{1,0:T(8,128)(2,1)S(1)}, bf16[2064,128]{1,0:T(8,128)(2,1)S(1)}, u32[]{:S(2)}, u32[]{:S(2)}) %collective-permute-start.3) | collective-permute-done | bytes 528416 | tf_op jit(solution)/shard_map/ppermute | solution.py:247
  29.7 5.7 %collective-permute-done.4.refs_1_ = bf16[2064,128]{1,0:T(8,128)(2,1)S(1)} collective-permute-done((bf16[2064,128]{1,0:T(8,128)(2,1)S(1)}, bf16[2064,128]{1,0:T(8,128)(2,1)S(1)}, u32[]{:S(2)}, u32[]{:S(2)}) %collective-permute-start.4) | collective-permute-done | bytes 528416 | tf_op jit(solution)/shard_map/ppermute | solution.py:251
  35.4 0.1 broadcast_select_fusion
  35.4 0.1 collective-permute-start.8
  35.5 0.5 collective-permute-start.6
  36.0 1.5 %collective-permute-start.5 = (bf16[2064,128]{1,0:T(8,128)(2,1)S(1)}, bf16[2064,128]{1,0:T(8,128)(2,1)S(1)}, u32[]{:S(2)}, u32[]{:S(2)}) collective-permute-start(bf16[2064,128]{1,0:T(8,128)(2,1)S(1)} %get-tuple-element.38), channel_id=1, source_target_pairs={{4,0},{6,2},{0,4},{2,6},{12,8},{14,10},{8,12},{10,14},{20,16},{22,... | collective-permute-start | bytes 1585160 | tf_op jit(solution)/shard_map/ppermute | solution.py:251
  37.5 0.0 collective-permute-done.7.refs_3_
  37.5 0.0 collective-permute-done.8.refs_5_
  37.5 0.7 %collective-permute-done.6.refs_2_ = bf16[2064,128]{1,0:T(8,128)(2,1)S(1)} collective-permute-done((bf16[2064,128]{1,0:T(8,128)(2,1)S(1)}, bf16[2064,128]{1,0:T(8,128)(2,1)S(1)}, u32[]{:S(2)}, u32[]{:S(2)}) %collective-permute-start.6) | collective-permute-done | bytes 528416 | tf_op jit(solution)/shard_map/ppermute | solution.py:251
  38.2 5.1 %shard_map.76.refs_3_ = f32[32,128,128]{2,1,0:T(8,128)S(1)} custom-call(s32[8,256]{1,0:T(8,128)S(1)} %shard_map.74.words_ref, bf16[4224,128]{1,0:T(8,128)(2,1)S(1)} %get-tuple-element.30.refs_0_, bf16[2064,128]{1,0:T(8,128)(2,1)S(1)} %collective-permute-done.4.refs_1_, bf16[2064,128]{1,0:T(8,128)(2,1)S(1)} %collective-permute-done.6.refs_2_, ...), custom_call_target="tpu_custom_call" | custom-call | flops 128 | bytes 128 | tf_op jit(solution)/shard_map/pallas_call | solution.py:44
  43.3 6.7 %collective-permute-done.5.refs_1_ = bf16[2064,128]{1,0:T(8,128)(2,1)S(1)} collective-permute-done((bf16[2064,128]{1,0:T(8,128)(2,1)S(1)}, bf16[2064,128]{1,0:T(8,128)(2,1)S(1)}, u32[]{:S(2)}, u32[]{:S(2)}) %collective-permute-start.5) | collective-permute-done | bytes 528416 | tf_op jit(solution)/shard_map/ppermute | solution.py:251
  50.0 0.0 collective-permute-start.9
  50.0 1.9 %collective-permute-done.9.refs_2_ = bf16[2064,128]{1,0:T(8,128)(2,1)S(1)} collective-permute-done((bf16[2064,128]{1,0:T(8,128)(2,1)S(1)}, bf16[2064,128]{1,0:T(8,128)(2,1)S(1)}, u32[]{:S(2)}, u32[]{:S(2)}) %collective-permute-start.9) | collective-permute-done | bytes 528416 | tf_op jit(solution)/shard_map/ppermute | solution.py:251
  51.9 5.1 %shard_map.77 = bf16[512,1024]{1,0:T(8,128)(2,1)} custom-call(s32[8,256]{1,0:T(8,128)S(1)} %shard_map.74.words_ref, bf16[4224,128]{1,0:T(8,128)(2,1)S(1)} %get-tuple-element.30.refs_0_, bf16[2064,128]{1,0:T(8,128)(2,1)S(1)} %collective-permute-done.5.refs_1_, bf16[2064,128]{1,0:T(8,128)(2,1)S(1)} %collective-permute-done.9.refs_2_, ...), custom_call_target="tpu_custom_call" | custom-call | flops 128 | bytes 128 | tf_op jit(solution)/shard_map/pallas_call | solution.py:44
Async XLA Ops:
  0.0 1.2 %copy-start = (bf16[1,1,32,128,128]{4,3,2,1,0:T(8,128)(2,1)S(1)}, bf16[1,1,32,128,128]{4,3,2,1,0:T(8,128)(2,1)}, u32[]{:S(2)}) copy-start(bf16[1,1,32,128,128]{4,3,2,1,0:T(8,128)(2,1)} %param.9) | copy-start | bytes 3145732
  1.2 0.7 %copy-start.2 = (s32[1,1,32]{2,1,0:T(1,128)S(1)}, s32[1,1,32]{2,1,0:T(1,128)}, u32[]{:S(2)}) copy-start(s32[1,1,32]{2,1,0:T(1,128)} %param.10) | copy-start | bytes 388
  1.9 23.3 %copy-start.1 = (bf16[1,1,16,128,128]{4,3,2,1,0:T(8,128)(2,1)S(1)}, bf16[1,1,16,128,128]{4,3,2,1,0:T(8,128)(2,1)}, u32[]{:S(2)}) copy-start(bf16[1,1,16,128,128]{4,3,2,1,0:T(8,128)(2,1)} %param.7) | copy-start | bytes 1572868
  2.0 21.5 %collective-permute-start = (bf16[2064,128]{1,0:T(8,128)(2,1)S(1)}, bf16[2064,128]{1,0:T(8,128)(2,1)S(1)}, u32[]{:S(2)}, u32[]{:S(2)}) collective-permute-start(bf16[2064,128]{1,0:T(8,128)(2,1)S(1)} %get-tuple-element.21.refs_2_), channel_id=1, source_target_pairs={{8,0},{10,2},{12,4},{14,6},{16,8},{18,10},{20,12},{22,14},{24,16},... | collective-permute-start | bytes 1585160 | tf_op jit(solution)/shard_map/ppermute | solution.py:247
  7.1 3.7 %collective-permute-start.1 = (s32[1,16]{1,0:T(1,128)}, s32[1,16]{1,0:T(1,128)S(1)}, u32[]{:S(2)}, u32[]{:S(2)}) collective-permute-start(s32[1,16]{1,0:T(1,128)} %bitcast.12), channel_id=1, source_target_pairs={{1,0},{0,1},{3,2},{2,3},{5,4},{4,5},{7,6},{6,7},{9,8},{8,9},{11,10... | collective-permute-start | bytes 200 | tf_op jit(solution)/shard_map/ppermute | solution.py:247
  10.8 12.7 %collective-permute-start.2 = (bf16[2048,128]{1,0:T(8,128)(2,1)}, bf16[2048,128]{1,0:T(8,128)(2,1)S(1)}, u32[]{:S(2)}, u32[]{:S(2)}) collective-permute-start(bf16[2048,128]{1,0:T(8,128)(2,1)} %bitcast.7), channel_id=1, source_target_pairs={{1,0},{0,1},{3,2},{2,3},{5,4},{4,5},{7,6},{6,7},{9,8},{8,9},{11,10... | collective-permute-start | bytes 1572872 | tf_op jit(solution)/shard_map/ppermute | solution.py:247
  12.3 17.4 %collective-permute-start.3 = (bf16[2064,128]{1,0:T(8,128)(2,1)S(1)}, bf16[2064,128]{1,0:T(8,128)(2,1)S(1)}, u32[]{:S(2)}, u32[]{:S(2)}) collective-permute-start(bf16[2064,128]{1,0:T(8,128)(2,1)S(1)} %get-tuple-element.28.refs_3_), channel_id=1, source_target_pairs={{8,0},{10,2},{12,4},{14,6},{16,8},{18,10},{20,12},{22,14},{24,16},... | collective-permute-start | bytes 1585160 | tf_op jit(solution)/shard_map/ppermute | solution.py:247
  13.6 0.7 %copy-start.3 = (s32[1,1,4]{2,1,0:T(1,128)S(1)}, s32[1,1,4]{2,1,0:T(1,128)}, u32[]{:S(2)}) copy-start(s32[1,1,4]{2,1,0:T(1,128)} %param.12) | copy-start | bytes 52
  14.2 0.7 %copy-start.4 = (s32[1,4]{1,0:T(1,128)S(1)}, s32[1,4]{1,0:T(1,128)}, u32[]{:S(2)}) copy-start(s32[1,4]{1,0:T(1,128)} %order_ref.1) | copy-start | bytes 52
  14.9 0.7 %copy-start.5 = (s32[1,1,16]{2,1,0:T(1,128)S(1)}, s32[1,1,16]{2,1,0:T(1,128)}, u32[]{:S(2)}) copy-start(s32[1,1,16]{2,1,0:T(1,128)} %param.8) | copy-start | bytes 196
  23.6 11.8 %collective-permute-start.4 = (bf16[2064,128]{1,0:T(8,128)(2,1)S(1)}, bf16[2064,128]{1,0:T(8,128)(2,1)S(1)}, u32[]{:S(2)}, u32[]{:S(2)}) collective-permute-start(bf16[2064,128]{1,0:T(8,128)(2,1)S(1)} %get-tuple-element.40), channel_id=1, source_target_pairs={{4,0},{6,2},{0,4},{2,6},{12,8},{14,10},{8,12},{10,14},{20,16},{22,... | collective-permute-start | bytes 1585160 | tf_op jit(solution)/shard_map/ppermute | solution.py:251
  25.2 12.4 %collective-permute-start.7 = (bf16[2064,128]{1,0:T(8,128)(2,1)S(1)}, bf16[2064,128]{1,0:T(8,128)(2,1)S(1)}, u32[]{:S(2)}, u32[]{:S(2)}) collective-permute-start(bf16[2064,128]{1,0:T(8,128)(2,1)S(1)} %get-tuple-element.39), channel_id=1, source_target_pairs={{2,0},{0,2},{6,4},{4,6},{10,8},{8,10},{14,12},{12,14},{18,16},{16,... | collective-permute-start | bytes 1585160 | tf_op jit(solution)/shard_map/ppermute | solution.py:251
  35.4 2.1 %collective-permute-start.8 = (bf16[2064,128]{1,0:T(8,128)(2,1)S(1)}, bf16[2064,128]{1,0:T(8,128)(2,1)S(1)}, u32[]{:S(2)}, u32[]{:S(2)}) collective-permute-start(bf16[2064,128]{1,0:T(8,128)(2,1)S(1)} %get-tuple-element.37), channel_id=1, source_target_pairs={{2,0},{0,2},{6,4},{4,6},{10,8},{8,10},{14,12},{12,14},{18,16},{16,... | collective-permute-start | bytes 1585160 | tf_op jit(solution)/shard_map/ppermute | solution.py:251
  35.5 2.7 %collective-permute-start.6 = (bf16[2064,128]{1,0:T(8,128)(2,1)S(1)}, bf16[2064,128]{1,0:T(8,128)(2,1)S(1)}, u32[]{:S(2)}, u32[]{:S(2)}) collective-permute-start(bf16[2064,128]{1,0:T(8,128)(2,1)S(1)} %collective-permute-done.4.refs_1_), channel_id=1, source_target_pairs={{2,0},{0,2},{6,4},{4,6},{10,8},{8,10},{14,12},{12,14},{18,16},{16,... | collective-permute-start | bytes 1585160 | tf_op jit(solution)/shard_map/ppermute | solution.py:251
  36.0 14.0 %collective-permute-start.5 = (bf16[2064,128]{1,0:T(8,128)(2,1)S(1)}, bf16[2064,128]{1,0:T(8,128)(2,1)S(1)}, u32[]{:S(2)}, u32[]{:S(2)}) collective-permute-start(bf16[2064,128]{1,0:T(8,128)(2,1)S(1)} %get-tuple-element.38), channel_id=1, source_target_pairs={{4,0},{6,2},{0,4},{2,6},{12,8},{14,10},{8,12},{10,14},{20,16},{22,... | collective-permute-start | bytes 1585160 | tf_op jit(solution)/shard_map/ppermute | solution.py:251
  50.0 1.9 %collective-permute-start.9 = (bf16[2064,128]{1,0:T(8,128)(2,1)S(1)}, bf16[2064,128]{1,0:T(8,128)(2,1)S(1)}, u32[]{:S(2)}, u32[]{:S(2)}) collective-permute-start(bf16[2064,128]{1,0:T(8,128)(2,1)S(1)} %collective-permute-done.5.refs_1_), channel_id=1, source_target_pairs={{2,0},{0,2},{6,4},{4,6},{10,8},{8,10},{14,12},{12,14},{18,16},{16,... | collective-permute-start | bytes 1585160 | tf_op jit(solution)/shard_map/ppermute | solution.py:251
where the time goes:
time: 57.5 us; the launch traced here: 57 us
  waiting for transfers between devices  24.9 us (43%)
  Pallas kernels  15 us (26%)
  starting transfers between devices  12.2 us (21%)
  local copies, waits for them, and re-layouts  4.67 us (8%)
    pallas_call x5, Pallas kernels, kernel_call(): pl.pallas_call(kernel, out_shape=out_shape, grid_spec=pltpu.PrefetchScala...  15 us
    ppermute x6, waiting for transfers between devices, swap(): return lax.ppermute(mine, 'row', [(i ^ bit, i) for i in range(n_row)])  14.9 us
    ppermute x4, waiting for transfers between devices, from_ahead(): lax.ppermute(block, axis, [((i + distance) % size, i) for i in range(size)])  9.96 us
    ppermute x4, starting transfers between devices, from_ahead(): lax.ppermute(block, axis, [((i + distance) % size, i) for i in range(size)])  8.59 us
    unnamed x12, local copies, waits for them, and re-layouts  3.85 us
    ppermute x6, starting transfers between devices, swap(): return lax.ppermute(mine, 'row', [(i ^ bit, i) for i in range(n_row)])  3.62 us
  transfers between devices with their start and end apart: 10, of which 7 were waited for; matrix products, arithmetic and copies ran while one was open for 2% of the time, Pallas kernels for 17%

commit v1 on v0

--- a/solution.py
+++ b/solution.py
@@ -9,8 +9,10 @@
 
 CCOLS = 8
 PARTS = 2
+FIRST_PART = 15, 32
 UNROLL = 16
-HEAD = 16
+HEAD = 32
+HEAD_STEP = 16
 VMEM_BYTES = 40 << 20
 VMEM = pl.BlockSpec(memory_space=pltpu.VMEM)
 
@@ -24,7 +26,9 @@
         self.n_stops, self.n_pairs, self.n_rows, self.n_col = n_stops, n_pairs, n_rows, n_col
         self.n_left, self.n_right, self.edge = n_left, n_right, edge
         self.parts = PARTS
-        self.per_part = n_right // PARTS
+        first = n_right * FIRST_PART[0] // FIRST_PART[1]
+        self.cuts = (0, first, n_right)
+        self.per_part = max(first, n_right - first)
         self.zero_slot = n_col * n_left
         self.row_bits = (n_rows - 1).bit_length()
         self.key_bits = self.row_bits + (self.per_part - 1).bit_length()
@@ -40,6 +44,7 @@
     scalars=(),
     scratch=(),
     specs=None,
+    flops=128,
 ):
     return pl.pallas_call(
         kernel,
@@ -51,48 +56,49 @@
             scratch_shapes=list(scratch),
         ),
         compiler_params=pltpu.CompilerParams(vmem_limit_bytes=VMEM_BYTES),
-        cost_estimate=pl.CostEstimate(flops=128, bytes_accessed=128, transcendentals=0),
+        cost_estimate=pl.CostEstimate(flops=flops, bytes_accessed=128, transcendentals=0),
     )(*scalars, *operands)
 
 
-def pack_kernel(blocks_ref, ids_ref, *refs):
+def pack_kernel(cuts, blocks_ref, ids_ref, *refs):
     part_refs, head_ref, sems = refs[:-2], refs[-2], refs[-1]
-    rows = blocks_ref.shape[0] // len(part_refs)
-    copies = [
-        pltpu.make_async_copy(
-            blocks_ref.at[pl.ds(part * rows, rows)], ref.at[pl.ds(HEAD, rows)], sems.at[part]
-        )
-        for part, ref in enumerate(part_refs)
-    ]
+    edge = blocks_ref.shape[1]
+    copies = []
+    for part, ref in enumerate(part_refs):
+        low, count = cuts[part] * edge, (cuts[part + 1] - cuts[part]) * edge
+        source, target = blocks_ref.at[pl.ds(low, count)], ref.at[pl.ds(HEAD, count)]
+        copies.append(pltpu.make_async_copy(source, target, sems.at[part]))
     for copy in copies:
         copy.start()
     head_ref[...] = jnp.zeros_like(head_ref)
     head_ref[0:1, : ids_ref.shape[1]] = ids_ref[...].astype(jnp.float32)
     for ref in part_refs:
-        ref[:HEAD, :] = head_ref[...].astype(ref.dtype)
+        for row in range(0, HEAD, HEAD_STEP):
+            ref[row : row + HEAD_STEP, :] = head_ref[...].astype(ref.dtype)
     for copy in copies:
         copy.wait()
 
 
-def pack(blocks, ids):
-    edge = blocks.shape[-1]
-    blocks = blocks.reshape(-1, edge)
-    shape = (HEAD + blocks.shape[0] // PARTS, edge)
+def pack(sizes, blocks, ids):
+    edge = sizes.edge
+    counts = [high - low for low, high in zip(sizes.cuts, sizes.cuts[1:])]
+    shapes = [(HEAD + count * edge, edge) for count in counts]
     return kernel_call(
-        pack_kernel,
-        [jax.ShapeDtypeStruct(shape, blocks.dtype)] * PARTS,
-        [blocks, ids.reshape(1, -1)],
-        scratch=[pltpu.VMEM((HEAD, edge), jnp.float32), pltpu.SemaphoreType.DMA((PARTS,))],
+        functools.partial(pack_kernel, sizes.cuts),
+        [jax.ShapeDtypeStruct(shape, blocks.dtype) for shape in shapes],
+        [blocks.reshape(-1, edge), ids.reshape(1, -1)],
+        scratch=[pltpu.VMEM((HEAD_STEP, edge), jnp.float32), pltpu.SemaphoreType.DMA((PARTS,))],
         specs=[pl.BlockSpec(memory_space=pl.ANY), VMEM],
     )
 
 
 def ids_of(ref):
-    return ref[:HEAD, :].astype(jnp.float32)[0:1, :]
+    return ref[:HEAD_STEP, :].astype(jnp.float32)[0:1, :]
 
 
 def prepare_kernel(sizes, count_ref, order_ref, pairs_ref, *refs):
-    id_refs, words_ref = refs[:-1], refs[-1]
+    words_ref = refs[-1]
+    id_sets = [ref[...] for ref in refs[:-1]]
     n_col, n_rows, parts = sizes.n_col, sizes.n_rows, sizes.parts
     n_pairs, width = sizes.n_pairs, sizes.width
 
@@ -101,7 +107,7 @@
 
     here = lax.axis_index("row")
     lane = lax.broadcasted_iota(jnp.int32, (n_pairs, 128), 1)
-    slot = lax.broadcasted_iota(jnp.int32, (n_pairs, sizes.n_left), 1)
+    slot = lane[:, : sizes.n_left]
     down = lax.broadcasted_iota(jnp.int32, (n_pairs, 1), 0)
     across = lax.broadcasted_iota(jnp.int32, (1, n_pairs), 1)
     places = lax.broadcasted_iota(jnp.int32, (1, width), 1).astype(jnp.float32)
@@ -110,9 +116,9 @@
     key_matrix = jnp.zeros((n_pairs, 128), jnp.float32)
     for stop in range(sizes.n_stops):
         ahead = lax.rem(here + stop, n_col)
-        ids = id_refs[0][...]
+        ids = id_sets[0]
         for j in range(1, n_col):
-            ids = jnp.where(ahead == j, id_refs[j][...], ids)
+            ids = jnp.where(ahead == j, id_sets[j], ids)
         left_row = jnp.zeros(ids.shape, jnp.float32)
         for i in range(n_rows):
             left_row = jnp.where(ids == i, order_ref[:, i : i + 1].astype(jnp.float32), left_row)
@@ -124,10 +130,10 @@
         keys.append(key)
         key_matrix = jnp.where(lane == stop, key, key_matrix)
     key_rows = key_matrix.T
-    cut = float(sizes.per_part * n_rows)
+    cut = float(sizes.cuts[1] * n_rows)
 
     def part_of(key):
-        return sum(jnp.where(key >= part * cut, 1.0, 0.0) for part in range(1, parts))
+        return jnp.where(key >= cut, 1.0, 0.0)
 
     scale = [float(1 << sizes.key_bits), float(1 << (sizes.key_bits + sizes.left_bits))]
     empty = sizes.zero_slot * (scale[0] + scale[1])
@@ -178,7 +184,7 @@
     core, col = lax.rem(lax.axis_index("row"), 2), lax.axis_index("col")
 
     def block(ref, slot, head):
-        return ref[pl.ds(pl.multiple_of(slot * edge + head, HEAD), edge), :]
+        return ref[pl.ds(pl.multiple_of(slot * edge + head, HEAD_STEP), edge), :]
 
     for array, head, part, ahead in layout:
         stop = jnp.where(
@@ -197,8 +203,8 @@
                 slot = (word & ((1 << sizes.key_bits) - 1)) >> sizes.row_bits
                 word = word >> sizes.key_bits
                 lefts = word & ((1 << sizes.left_bits) - 1), word >> sizes.left_bits
-                target = row * CCOLS + col_ref[array, slot + part * sizes.per_part]
-                right = block(right_refs[array], slot, head + HEAD)
+                target = row * CCOLS + col_ref[array, slot + sizes.cuts[part]]
+                right = block(right_refs[array], slot, head)
                 total_ref[target] += jnp.dot(
                     jnp.concatenate([block(left_ref, left, 0) for left in lefts], axis=1),
                     jnp.concatenate([right, right], axis=0),
@@ -246,8 +252,9 @@
         size = lax.axis_size(axis)
         return lax.ppermute(block, axis, [((i + distance) % size, i) for i in range(size)])
 
-    def swap(bit, lower, upper):
+    def swap(bit, lower, upper, skip=0):
         mine = lower if lower is upper else jnp.where(row // bit % 2 == 1, upper, lower)
+        mine = mine[skip:]
         return lax.ppermute(mine, "row", [(i ^ bit, i) for i in range(n_row)])
 
     def both(distance):
@@ -257,17 +264,17 @@
         ahead = 2 * j + 1, 2 * j - 1
         return tuple(d if 1 <= d <= reach else None for d in ahead)
 
-    left_ids = [a_rows.reshape(1, -1)]
-    left_ids += [from_ahead(left_ids[0], "col", j) for j in range(1, n_col)]
-    own = list(pack(b_blocks, b_cols))
+    own = pack(sizes, b_blocks, b_cols)
     even = {j: [from_ahead(part, "row", 2 * j) for part in own] for j in range(2, chips + 2, 2)}
-    left_own, left_ids = lax.optimization_barrier((a_blocks.reshape(-1, edge), left_ids))
+    left_ids, left_own = a_rows.reshape(1, -1), a_blocks.reshape(-1, edge)
+    left_ids = [left_ids] + [from_ahead(left_ids, "col", j) for j in range(1, n_col)]
     lefts = [left_own] + [from_ahead(left_own, "col", j) for j in range(1, n_col)]
     words = kernel_call(
         functools.partial(prepare_kernel, sizes),
         jax.ShapeDtypeStruct((PARTS * n_stops, sizes.width), jnp.int32),
         [pair_count.reshape(1, -1), row_order, pair_list.reshape(2 * n_stops, n_pairs).T]
         + left_ids,
+        flops=1 << 34,
     )
 
     def wait(part, *others):
@@ -290,7 +297,7 @@
             out_shape = jax.ShapeDtypeStruct(sums, jnp.float32)
         if total is None:
             left_shape = ((sizes.zero_slot + 1) * edge, edge)
-            out_shape = [out_shape, jax.ShapeDtypeStruct(left_shape, left_own.dtype)]
+            out_shape = [out_shape, jax.ShapeDtypeStruct(left_shape, b_blocks.dtype)]
         lines = round_up(len(rights), 8)
         return kernel_call(
             functools.partial(
@@ -310,45 +317,27 @@
         )
 
     def pieces_of(j, part, block):
-        pieces = [(block, 0, part, both(2 * j))]
-        if j < chips:
-            pieces.append((swap(1, block, block), 0, part, swapped(j)))
-        return pieces
-
-    def odd_pieces(part):
-        return [piece for j in odds for piece in pieces_of(j, part, odd[part][j])]
-
-    def even_pieces(part):
-        return [piece for j in evens for piece in pieces_of(j, part, even[j][part])]
-
-    def end_pieces(part):
-        farthest = odd[part][chips] if chips % 2 else even[chips][part]
-        ahead = swapped(0)[0], swapped(chips)[1]
-        return [(swap(1, farthest, own[part]), 0, part, ahead)]
-
-    def even_and_end(parts):
-        pieces = []
-        for part in parts:
-            pieces += even_pieces(part) + ([] if chips % 2 else end_pieces(part))
-        return pieces
-
-    def odd_and_end(parts):
-        pieces = []
-        for part in parts:
-            pieces += odd_pieces(part) + (end_pieces(part) if chips % 2 else [])
-        return pieces
+        skip = HEAD_STEP if j in evens else 0
+        theirs = swap(1, block, block, skip)
+        return [
+            (block, HEAD, part, both(2 * j)),
+            (theirs, HEAD - skip, part, swapped(j)),
+        ]
 
     odd = {}
     words, lefts = wait(0, words, lefts)
     odd[0] = pass_on(0)
-    pieces = [(own[part], 0, part, both(0)) for part in parts]
-    total, left_all = add(None, pieces + even_pieces(0))
+    pieces = [piece for part in parts for piece in pieces_of(0, part, own[part])]
+    pieces += [piece for j in evens for piece in pieces_of(j, 0, even[j][0])]
+    total, left_all = add(None, pieces)
     odd[0], total = wait(1, odd[0], total)
     odd[1] = pass_on(1)
-    ends = [] if chips % 2 else end_pieces(0)
-    total = add(total, odd_and_end((0,)) + ends + even_and_end((1,)))
+    pieces = [piece for j in odds for piece in pieces_of(j, 0, odd[0][j])]
+    pieces += [piece for j in evens for piece in pieces_of(j, 1, even[j][1])]
+    total = add(total, pieces)
     odd[1], total = lax.optimization_barrier((odd[1], total))
-    return add(total, odd_and_end((1,)), closes=True)
+    pieces = [piece for j in odds for piece in pieces_of(j, 1, odd[1][j])]
+    return add(total, pieces, closes=True)
 
 
 def solution(mesh):

time: 57.5 us -> 57.5 us (level)
  the two profiles are of different devices: /device:TPU:0 before, /device:TPU:7 now
where the time goes in v1:
time: 57.5 us; the launch traced here: 57.4 us
  Pallas kernels  23.1 us (40%)
  waiting for transfers between devices  16.8 us (29%)
  starting transfers between devices  12.5 us (22%)
  local copies, waits for them, and re-layouts  4.75 us (8%)
    pallas_call x5, Pallas kernels, kernel_call(): pl.pallas_call(kernel, out_shape=out_shape, grid_spec=pltpu.PrefetchScala...  23.1 us
    ppermute x4, waiting for transfers between devices, from_ahead(): lax.ppermute(block, axis, [((i + distance) % size, i) for i in range(size)])  9.47 us
    ppermute x8, starting transfers between devices, swap(): return lax.ppermute(mine, 'row', [(i ^ bit, i) for i in range(n_row)])  8.55 us
    ppermute x8, waiting for transfers between devices, swap(): return lax.ppermute(mine, 'row', [(i ^ bit, i) for i in range(n_row)])  7.34 us
    ppermute x4, starting transfers between devices, from_ahead(): lax.ppermute(block, axis, [((i + distance) % size, i) for i in range(size)])  3.94 us
    unnamed x12, local copies, waits for them, and re-layouts  3.85 us
  transfers between devices with their start and end apart: 12, of which 7 were waited for; matrix products, arithmetic and copies ran while one was open for 2% of the time, Pallas kernels for 28%

profile of v1, /device:TPU:7, one launch (start us, length us, event | category | flops | bytes accessed | tf_op | source)
XLA Modules:
  0.0 57.4 jit_solution(17632521672822597453)
XLA Ops:
  0.0 0.0 copy-start
  0.0 1.2 %copy-done = bf16[1,1,32,128,128]{4,3,2,1,0:T(8,128)(2,1)S(1)} copy-done((bf16[1,1,32,128,128]{4,3,2,1,0:T(8,128)(2,1)S(1)}, bf16[1,1,32,128,128]{4,3,2,1,0:T(8,128)(2,1)}, u32[]{:S(2)}) %copy-start) | copy-done | bytes 1048600
  1.2 0.0 copy-start.2
  1.2 0.7 %copy-done.2 = s32[1,1,32]{2,1,0:T(1,128)S(1)} copy-done((s32[1,1,32]{2,1,0:T(1,128)S(1)}, s32[1,1,32]{2,1,0:T(1,128)}, u32[]{:S(2)}) %copy-start.2) | copy-done | bytes 152
  1.9 0.4 shard_map.73
  2.3 0.7 %collective-permute-start.3 = (bf16[1952,128]{1,0:T(8,128)(2,1)S(1)}, bf16[1952,128]{1,0:T(8,128)(2,1)S(1)}, u32[]{:S(2)}, u32[]{:S(2)}) collective-permute-start(bf16[1952,128]{1,0:T(8,128)(2,1)S(1)} %get-tuple-element.18.refs_2_), channel_id=1, source_target_pairs={{2,0},{0,2},{6,4},{4,6},{10,8},{8,10},{14,12},{12,14},{18,16},{16,... | collective-permute-start | bytes 1499144 | tf_op jit(solution)/shard_map/ppermute | solution.py:258
  3.0 3.3 %collective-permute-start = (bf16[1952,128]{1,0:T(8,128)(2,1)S(1)}, bf16[1952,128]{1,0:T(8,128)(2,1)S(1)}, u32[]{:S(2)}, u32[]{:S(2)}) collective-permute-start(bf16[1952,128]{1,0:T(8,128)(2,1)S(1)} %get-tuple-element.18.refs_2_), channel_id=1, source_target_pairs={{8,0},{10,2},{12,4},{14,6},{16,8},{18,10},{20,12},{22,14},{24,16},... | collective-permute-start | bytes 1499144 | tf_op jit(solution)/shard_map/ppermute | solution.py:253
  6.4 0.2 collective-permute-start.6
  6.5 0.6 %collective-permute-start.4 = (bf16[2208,128]{1,0:T(8,128)(2,1)S(1)}, bf16[2208,128]{1,0:T(8,128)(2,1)S(1)}, u32[]{:S(2)}, u32[]{:S(2)}) collective-permute-start(bf16[2208,128]{1,0:T(8,128)(2,1)S(1)} %get-tuple-element.22.refs_4_), channel_id=1, source_target_pairs={{2,0},{0,2},{6,4},{4,6},{10,8},{8,10},{14,12},{12,14},{18,16},{16,... | collective-permute-start | bytes 1695752 | tf_op jit(solution)/shard_map/ppermute | solution.py:258
  7.2 0.2 collective-permute-start.1
  7.4 0.7 %reshape.21 = s32[8,256]{1,0:T(8,128)S(1)} reshape(s32[1,1,4,2,256]{4,3,2,1,0:T(2,128)} %param.11) | data formatting | bytes 16384 | tf_op jit(solution)/shard_map/reshape | solution.py:275
  8.1 0.1 copy.9
  8.2 1.8 %collective-permute-done.1.refs_1_ = s32[1,16]{1,0:T(1,128)S(1)} collective-permute-done((s32[1,16]{1,0:T(1,128)}, s32[1,16]{1,0:T(1,128)S(1)}, u32[]{:S(2)}, u32[]{:S(2)}) %collective-permute-start.1) | collective-permute-done | bytes 96 | tf_op jit(solution)/shard_map/ppermute | solution.py:253
  10.0 0.2 collective-permute-start.2
  10.2 0.0 copy-start.3
  10.2 0.7 %copy-done.3 = s32[1,1,4]{2,1,0:T(1,128)S(1)} copy-done((s32[1,1,4]{2,1,0:T(1,128)S(1)}, s32[1,1,4]{2,1,0:T(1,128)}, u32[]{:S(2)}) %copy-start.3) | copy-done | bytes 40
  10.9 0.0 copy-start.4
  10.9 0.7 %copy-done.4 = s32[1,4]{1,0:T(1,128)S(1)} copy-done((s32[1,4]{1,0:T(1,128)S(1)}, s32[1,4]{1,0:T(1,128)}, u32[]{:S(2)}) %copy-start.4) | copy-done | bytes 40
  11.5 0.0 copy-start.5
  11.5 0.7 %copy-done.5 = s32[1,1,16]{2,1,0:T(1,128)S(1)} copy-done((s32[1,1,16]{2,1,0:T(1,128)S(1)}, s32[1,1,16]{2,1,0:T(1,128)}, u32[]{:S(2)}) %copy-start.5) | copy-done | bytes 88
  12.2 2.9 %shard_map.74.words_ref = s32[8,256]{1,0:T(8,128)S(1)} custom-call(s32[1,4]{1,0:T(1,128)S(1)} %bitcast.11, s32[1,4]{1,0:T(1,128)S(1)} %copy-done.4, s32[256,8]{1,0:T(8,128)S(1)} %bitcast.9, s32[1,16]{1,0:T(1,128)S(1)} %bitcast.13, s32[1,16]{1,0:T(1,128)S(1)} %collective-permute-done.1.refs_1_), custom_call_target="tpu_custom_call" | custom-call | flops 17179869184 | bytes 128 | tf_op jit(solution)/shard_map/pallas_call | solution.py:49
  15.0 0.0 copy-start.1
  15.1 2.1 %collective-permute-done.refs_6_ = bf16[1952,128]{1,0:T(8,128)(2,1)S(1)} collective-permute-done((bf16[1952,128]{1,0:T(8,128)(2,1)S(1)}, bf16[1952,128]{1,0:T(8,128)(2,1)S(1)}, u32[]{:S(2)}, u32[]{:S(2)}) %collective-permute-start) | collective-permute-done | bytes 499744 | tf_op jit(solution)/shard_map/ppermute | solution.py:253
  17.1 5.6 %collective-permute-done.2.refs_1_ = bf16[2048,128]{1,0:T(8,128)(2,1)S(1)} collective-permute-done((bf16[2048,128]{1,0:T(8,128)(2,1)}, bf16[2048,128]{1,0:T(8,128)(2,1)S(1)}, u32[]{:S(2)}, u32[]{:S(2)}) %collective-permute-start.2) | collective-permute-done | bytes 524320 | tf_op jit(solution)/shard_map/ppermute | solution.py:253
  22.8 0.1 broadcast_select_fusion.1
  22.8 0.3 collective-permute-start.7
  23.2 2.1 %collective-permute-start.5 = (bf16[1936,128]{1,0:T(8,128)(2,1)S(1)}, bf16[1936,128]{1,0:T(8,128)(2,1)S(1)}, u32[]{:S(2)}, u32[]{:S(2)}) collective-permute-start(bf16[1936,128]{1,0:T(8,128)(2,1)S(1)} %slice.6), channel_id=1, source_target_pairs={{2,0},{0,2},{6,4},{4,6},{10,8},{8,10},{14,12},{12,14},{18,16},{16,... | collective-permute-start | bytes 1486856 | tf_op jit(solution)/shard_map/ppermute | solution.py:258
  25.3 0.0 collective-permute-done.3.refs_3_
  25.3 0.0 collective-permute-done.4.refs_5_
  25.3 1.5 %collective-permute-done.5.refs_7_ = bf16[1936,128]{1,0:T(8,128)(2,1)S(1)} collective-permute-done((bf16[1936,128]{1,0:T(8,128)(2,1)S(1)}, bf16[1936,128]{1,0:T(8,128)(2,1)S(1)}, u32[]{:S(2)}, u32[]{:S(2)}) %collective-permute-start.5) | collective-permute-done | bytes 495648 | tf_op jit(solution)/shard_map/ppermute | solution.py:258
  26.8 0.0 copy-done.1
  26.8 5.2 %shard_map.75 = (f32[32,128,128]{2,1,0:T(8,128)S(1)}, bf16[4224,128]{1,0:T(8,128)(2,1)S(1)}) custom-call(s32[8,256]{1,0:T(8,128)S(1)} %shard_map.74.words_ref, bf16[2048,128]{1,0:T(8,128)(2,1)S(1)} %bitcast.8, bf16[2048,128]{1,0:T(8,128)(2,1)S(1)} %collective-permute-done.2.refs_1_, bf16[1952,128]{1,0:T(8,128)(2,1)S(1)} %get-tuple-element.18.refs_2_, ...), custom_call_target="tpu_custom_call" | custom-call | flops 128 | bytes 128 | tf_op jit(solution)/shard_map/pallas_call | solution.py:49
  32.0 0.0 collective-permute-done.6.refs_3_
  32.0 2.0 %collective-permute-done.7.refs_1_ = bf16[1952,128]{1,0:T(8,128)(2,1)S(1)} collective-permute-done((bf16[1952,128]{1,0:T(8,128)(2,1)S(1)}, bf16[1952,128]{1,0:T(8,128)(2,1)S(1)}, u32[]{:S(2)}, u32[]{:S(2)}) %collective-permute-start.7) | collective-permute-done | bytes 499744 | tf_op jit(solution)/shard_map/ppermute | solution.py:258
  34.0 0.1 broadcast_select_fusion
  34.1 0.3 collective-permute-start.8
  34.5 3.0 %collective-permute-start.10 = (bf16[2192,128]{1,0:T(8,128)(2,1)S(1)}, bf16[2192,128]{1,0:T(8,128)(2,1)S(1)}, u32[]{:S(2)}, u32[]{:S(2)}) collective-permute-start(bf16[2192,128]{1,0:T(8,128)(2,1)S(1)} %slice.7), channel_id=1, source_target_pairs={{2,0},{0,2},{6,4},{4,6},{10,8},{8,10},{14,12},{12,14},{18,16},{16,... | collective-permute-start | bytes 1683464 | tf_op jit(solution)/shard_map/ppermute | solution.py:258
  37.5 0.1 collective-permute-start.9
  37.6 2.2 %collective-permute-done.9.refs_2_ = bf16[1952,128]{1,0:T(8,128)(2,1)S(1)} collective-permute-done((bf16[1952,128]{1,0:T(8,128)(2,1)S(1)}, bf16[1952,128]{1,0:T(8,128)(2,1)S(1)}, u32[]{:S(2)}, u32[]{:S(2)}) %collective-permute-start.9) | collective-permute-done | bytes 499744 | tf_op jit(solution)/shard_map/ppermute | solution.py:258
  39.8 0.0 collective-permute-done.10.refs_4_
  39.8 8.2 %shard_map.76.refs_3_ = f32[32,128,128]{2,1,0:T(8,128)S(1)} custom-call(s32[8,256]{1,0:T(8,128)S(1)} %shard_map.74.words_ref, bf16[4224,128]{1,0:T(8,128)(2,1)S(1)} %get-tuple-element.24.refs_0_, bf16[1952,128]{1,0:T(8,128)(2,1)S(1)} %collective-permute-done.7.refs_1_, bf16[1952,128]{1,0:T(8,128)(2,1)S(1)} %collective-permute-done.9.refs_2_, ...), custom_call_target="tpu_custom_call" | custom-call | flops 128 | bytes 128 | tf_op jit(solution)/shard_map/pallas_call | solution.py:49
  48.0 0.0 collective-permute-done.8.refs_1_
  48.0 1.3 %collective-permute-start.11 = (bf16[2208,128]{1,0:T(8,128)(2,1)S(1)}, bf16[2208,128]{1,0:T(8,128)(2,1)S(1)}, u32[]{:S(2)}, u32[]{:S(2)}) collective-permute-start(bf16[2208,128]{1,0:T(8,128)(2,1)S(1)} %collective-permute-done.8.refs_1_), channel_id=1, source_target_pairs={{2,0},{0,2},{6,4},{4,6},{10,8},{8,10},{14,12},{12,14},{18,16},{16,... | collective-permute-start | bytes 1695752 | tf_op jit(solution)/shard_map/ppermute | solution.py:258
  49.4 1.6 %collective-permute-done.11.refs_2_ = bf16[2208,128]{1,0:T(8,128)(2,1)S(1)} collective-permute-done((bf16[2208,128]{1,0:T(8,128)(2,1)S(1)}, bf16[2208,128]{1,0:T(8,128)(2,1)S(1)}, u32[]{:S(2)}, u32[]{:S(2)}) %collective-permute-start.11) | collective-permute-done | bytes 565280 | tf_op jit(solution)/shard_map/ppermute | solution.py:258
  51.0 6.4 %shard_map.77 = bf16[512,1024]{1,0:T(8,128)(2,1)} custom-call(s32[8,256]{1,0:T(8,128)S(1)} %shard_map.74.words_ref, bf16[4224,128]{1,0:T(8,128)(2,1)S(1)} %get-tuple-element.24.refs_0_, bf16[2208,128]{1,0:T(8,128)(2,1)S(1)} %collective-permute-done.8.refs_1_, bf16[2208,128]{1,0:T(8,128)(2,1)S(1)} %collective-permute-done.11.refs_2_, ...), custom_call_target="tpu_custom_call" | custom-call | flops 128 | bytes 128 | tf_op jit(solution)/shard_map/pallas_call | solution.py:49
  (2 shorter events, 0.1 us)
Async XLA Ops:
  0.0 1.2 %copy-start = (bf16[1,1,32,128,128]{4,3,2,1,0:T(8,128)(2,1)S(1)}, bf16[1,1,32,128,128]{4,3,2,1,0:T(8,128)(2,1)}, u32[]{:S(2)}) copy-start(bf16[1,1,32,128,128]{4,3,2,1,0:T(8,128)(2,1)} %param.9) | copy-start | bytes 3145732
  1.2 0.7 %copy-start.2 = (s32[1,1,32]{2,1,0:T(1,128)S(1)}, s32[1,1,32]{2,1,0:T(1,128)}, u32[]{:S(2)}) copy-start(s32[1,1,32]{2,1,0:T(1,128)} %param.10) | copy-start | bytes 388
  2.3 23.0 %collective-permute-start.3 = (bf16[1952,128]{1,0:T(8,128)(2,1)S(1)}, bf16[1952,128]{1,0:T(8,128)(2,1)S(1)}, u32[]{:S(2)}, u32[]{:S(2)}) collective-permute-start(bf16[1952,128]{1,0:T(8,128)(2,1)S(1)} %get-tuple-element.18.refs_2_), channel_id=1, source_target_pairs={{2,0},{0,2},{6,4},{4,6},{10,8},{8,10},{14,12},{12,14},{18,16},{16,... | collective-permute-start | bytes 1499144 | tf_op jit(solution)/shard_map/ppermute | solution.py:258
  3.0 14.1 %collective-permute-start = (bf16[1952,128]{1,0:T(8,128)(2,1)S(1)}, bf16[1952,128]{1,0:T(8,128)(2,1)S(1)}, u32[]{:S(2)}, u32[]{:S(2)}) collective-permute-start(bf16[1952,128]{1,0:T(8,128)(2,1)S(1)} %get-tuple-element.18.refs_2_), channel_id=1, source_target_pairs={{8,0},{10,2},{12,4},{14,6},{16,8},{18,10},{20,12},{22,14},{24,16},... | collective-permute-start | bytes 1499144 | tf_op jit(solution)/shard_map/ppermute | solution.py:253
  6.4 25.6 %collective-permute-start.6 = (bf16[2208,128]{1,0:T(8,128)(2,1)S(1)}, bf16[2208,128]{1,0:T(8,128)(2,1)S(1)}, u32[]{:S(2)}, u32[]{:S(2)}) collective-permute-start(bf16[2208,128]{1,0:T(8,128)(2,1)S(1)} %get-tuple-element.22.refs_4_), channel_id=1, source_target_pairs={{8,0},{10,2},{12,4},{14,6},{16,8},{18,10},{20,12},{22,14},{24,16},... | collective-permute-start | bytes 1695752 | tf_op jit(solution)/shard_map/ppermute | solution.py:253
  6.5 18.8 %collective-permute-start.4 = (bf16[2208,128]{1,0:T(8,128)(2,1)S(1)}, bf16[2208,128]{1,0:T(8,128)(2,1)S(1)}, u32[]{:S(2)}, u32[]{:S(2)}) collective-permute-start(bf16[2208,128]{1,0:T(8,128)(2,1)S(1)} %get-tuple-element.22.refs_4_), channel_id=1, source_target_pairs={{2,0},{0,2},{6,4},{4,6},{10,8},{8,10},{14,12},{12,14},{18,16},{16,... | collective-permute-start | bytes 1695752 | tf_op jit(solution)/shard_map/ppermute | solution.py:258
  7.2 2.8 %collective-permute-start.1 = (s32[1,16]{1,0:T(1,128)}, s32[1,16]{1,0:T(1,128)S(1)}, u32[]{:S(2)}, u32[]{:S(2)}) collective-permute-start(s32[1,16]{1,0:T(1,128)} %bitcast.12), channel_id=1, source_target_pairs={{1,0},{0,1},{3,2},{2,3},{5,4},{4,5},{7,6},{6,7},{9,8},{8,9},{11,10... | collective-permute-start | bytes 200 | tf_op jit(solution)/shard_map/ppermute | solution.py:253
  10.0 12.8 %collective-permute-start.2 = (bf16[2048,128]{1,0:T(8,128)(2,1)}, bf16[2048,128]{1,0:T(8,128)(2,1)S(1)}, u32[]{:S(2)}, u32[]{:S(2)}) collective-permute-start(bf16[2048,128]{1,0:T(8,128)(2,1)} %bitcast.7), channel_id=1, source_target_pairs={{1,0},{0,1},{3,2},{2,3},{5,4},{4,5},{7,6},{6,7},{9,8},{8,9},{11,10... | collective-permute-start | bytes 1572872 | tf_op jit(solution)/shard_map/ppermute | solution.py:253
  10.2 0.7 %copy-start.3 = (s32[1,1,4]{2,1,0:T(1,128)S(1)}, s32[1,1,4]{2,1,0:T(1,128)}, u32[]{:S(2)}) copy-start(s32[1,1,4]{2,1,0:T(1,128)} %param.12) | copy-start | bytes 52
  10.9 0.7 %copy-start.4 = (s32[1,4]{1,0:T(1,128)S(1)}, s32[1,4]{1,0:T(1,128)}, u32[]{:S(2)}) copy-start(s32[1,4]{1,0:T(1,128)} %order_ref.1) | copy-start | bytes 52
  11.5 0.7 %copy-start.5 = (s32[1,1,16]{2,1,0:T(1,128)S(1)}, s32[1,1,16]{2,1,0:T(1,128)}, u32[]{:S(2)}) copy-start(s32[1,1,16]{2,1,0:T(1,128)} %param.8) | copy-start | bytes 196
  15.0 11.7 %copy-start.1 = (bf16[1,1,16,128,128]{4,3,2,1,0:T(8,128)(2,1)S(1)}, bf16[1,1,16,128,128]{4,3,2,1,0:T(8,128)(2,1)}, u32[]{:S(2)}) copy-start(bf16[1,1,16,128,128]{4,3,2,1,0:T(8,128)(2,1)} %param.7) | copy-start | bytes 1572868
  22.8 11.2 %collective-permute-start.7 = (bf16[1952,128]{1,0:T(8,128)(2,1)S(1)}, bf16[1952,128]{1,0:T(8,128)(2,1)S(1)}, u32[]{:S(2)}, u32[]{:S(2)}) collective-permute-start(bf16[1952,128]{1,0:T(8,128)(2,1)S(1)} %broadcast_select_fusion.1), channel_id=1, source_target_pairs={{4,0},{6,2},{0,4},{2,6},{12,8},{14,10},{8,12},{10,14},{20,16},{22,... | collective-permute-start | bytes 1499144 | tf_op jit(solution)/shard_map/ppermute | solution.py:258
  23.2 3.6 %collective-permute-start.5 = (bf16[1936,128]{1,0:T(8,128)(2,1)S(1)}, bf16[1936,128]{1,0:T(8,128)(2,1)S(1)}, u32[]{:S(2)}, u32[]{:S(2)}) collective-permute-start(bf16[1936,128]{1,0:T(8,128)(2,1)S(1)} %slice.6), channel_id=1, source_target_pairs={{2,0},{0,2},{6,4},{4,6},{10,8},{8,10},{14,12},{12,14},{18,16},{16,... | collective-permute-start | bytes 1486856 | tf_op jit(solution)/shard_map/ppermute | solution.py:258
  34.1 13.9 %collective-permute-start.8 = (bf16[2208,128]{1,0:T(8,128)(2,1)S(1)}, bf16[2208,128]{1,0:T(8,128)(2,1)S(1)}, u32[]{:S(2)}, u32[]{:S(2)}) collective-permute-start(bf16[2208,128]{1,0:T(8,128)(2,1)S(1)} %broadcast_select_fusion), channel_id=1, source_target_pairs={{4,0},{6,2},{0,4},{2,6},{12,8},{14,10},{8,12},{10,14},{20,16},{22,... | collective-permute-start | bytes 1695752 | tf_op jit(solution)/shard_map/ppermute | solution.py:258
  34.5 5.3 %collective-permute-start.10 = (bf16[2192,128]{1,0:T(8,128)(2,1)S(1)}, bf16[2192,128]{1,0:T(8,128)(2,1)S(1)}, u32[]{:S(2)}, u32[]{:S(2)}) collective-permute-start(bf16[2192,128]{1,0:T(8,128)(2,1)S(1)} %slice.7), channel_id=1, source_target_pairs={{2,0},{0,2},{6,4},{4,6},{10,8},{8,10},{14,12},{12,14},{18,16},{16,... | collective-permute-start | bytes 1683464 | tf_op jit(solution)/shard_map/ppermute | solution.py:258
  37.5 2.3 %collective-permute-start.9 = (bf16[1952,128]{1,0:T(8,128)(2,1)S(1)}, bf16[1952,128]{1,0:T(8,128)(2,1)S(1)}, u32[]{:S(2)}, u32[]{:S(2)}) collective-permute-start(bf16[1952,128]{1,0:T(8,128)(2,1)S(1)} %collective-permute-done.7.refs_1_), channel_id=1, source_target_pairs={{2,0},{0,2},{6,4},{4,6},{10,8},{8,10},{14,12},{12,14},{18,16},{16,... | collective-permute-start | bytes 1499144 | tf_op jit(solution)/shard_map/ppermute | solution.py:258
  48.0 2.9 %collective-permute-start.11 = (bf16[2208,128]{1,0:T(8,128)(2,1)S(1)}, bf16[2208,128]{1,0:T(8,128)(2,1)S(1)}, u32[]{:S(2)}, u32[]{:S(2)}) collective-permute-start(bf16[2208,128]{1,0:T(8,128)(2,1)S(1)} %collective-permute-done.8.refs_1_), channel_id=1, source_target_pairs={{2,0},{0,2},{6,4},{4,6},{10,8},{8,10},{14,12},{12,14},{18,16},{16,... | collective-permute-start | bytes 1695752 | tf_op jit(solution)/shard_map/ppermute | solution.py:258

commit v2 on v1

--- a/solution.py
+++ b/solution.py
@@ -8,10 +8,10 @@
 from jax.sharding import PartitionSpec as P
 
 CCOLS = 8
-PARTS = 2
-FIRST_PART = 15, 32
+SHARES = (10, 21, 32)
+PARTS = len(SHARES)
 UNROLL = 16
-HEAD = 32
+HEADS = (32, 32, 48)
 HEAD_STEP = 16
 VMEM_BYTES = 40 << 20
 VMEM = pl.BlockSpec(memory_space=pltpu.VMEM)
@@ -26,9 +26,8 @@
         self.n_stops, self.n_pairs, self.n_rows, self.n_col = n_stops, n_pairs, n_rows, n_col
         self.n_left, self.n_right, self.edge = n_left, n_right, edge
         self.parts = PARTS
-        first = n_right * FIRST_PART[0] // FIRST_PART[1]
-        self.cuts = (0, first, n_right)
-        self.per_part = max(first, n_right - first)
+        self.cuts = (0, *(n_right * share // SHARES[-1] for share in SHARES))
+        self.per_part = max(high - low for low, high in zip(self.cuts, self.cuts[1:]))
         self.zero_slot = n_col * n_left
         self.row_bits = (n_rows - 1).bit_length()
         self.key_bits = self.row_bits + (self.per_part - 1).bit_length()
@@ -66,14 +65,14 @@
     copies = []
     for part, ref in enumerate(part_refs):
         low, count = cuts[part] * edge, (cuts[part + 1] - cuts[part]) * edge
-        source, target = blocks_ref.at[pl.ds(low, count)], ref.at[pl.ds(HEAD, count)]
+        source, target = blocks_ref.at[pl.ds(low, count)], ref.at[pl.ds(HEADS[part], count)]
         copies.append(pltpu.make_async_copy(source, target, sems.at[part]))
     for copy in copies:
         copy.start()
     head_ref[...] = jnp.zeros_like(head_ref)
     head_ref[0:1, : ids_ref.shape[1]] = ids_ref[...].astype(jnp.float32)
-    for ref in part_refs:
-        for row in range(0, HEAD, HEAD_STEP):
+    for head, ref in zip(HEADS, part_refs):
+        for row in range(0, head, HEAD_STEP):
             ref[row : row + HEAD_STEP, :] = head_ref[...].astype(ref.dtype)
     for copy in copies:
         copy.wait()
@@ -82,7 +81,7 @@
 def pack(sizes, blocks, ids):
     edge = sizes.edge
     counts = [high - low for low, high in zip(sizes.cuts, sizes.cuts[1:])]
-    shapes = [(HEAD + count * edge, edge) for count in counts]
+    shapes = [(head + count * edge, edge) for head, count in zip(HEADS, counts)]
     return kernel_call(
         functools.partial(pack_kernel, sizes.cuts),
         [jax.ShapeDtypeStruct(shape, blocks.dtype) for shape in shapes],
@@ -130,10 +129,16 @@
         keys.append(key)
         key_matrix = jnp.where(lane == stop, key, key_matrix)
     key_rows = key_matrix.T
-    cut = float(sizes.cuts[1] * n_rows)
+    cuts = [float(cut * n_rows) for cut in sizes.cuts]
 
     def part_of(key):
-        return jnp.where(key >= cut, 1.0, 0.0)
+        return sum(jnp.where(key >= cut, 1.0, 0.0) for cut in cuts[1:-1])
+
+    def start_of(key):
+        low = jnp.zeros_like(key)
+        for cut in cuts[1:-1]:
+            low = jnp.where(key >= cut, cut, low)
+        return low
 
     scale = [float(1 << sizes.key_bits), float(1 << (sizes.key_bits + sizes.left_bits))]
     empty = sizes.zero_slot * (scale[0] + scale[1])
@@ -147,7 +152,7 @@
         group = jnp.floor(rank * 0.5)
         opens = rank == 2.0 * group
         group += total((other < key) & (own_part == other_part) & other_opens, 1.0, 1)
-        word = jnp.where(opens, left * scale[0] + key - own_part * cut, left * scale[1])
+        word = jnp.where(opens, left * scale[0] + key - start_of(key), left * scale[1])
         for part in range(parts):
             counted = (own_part == float(part)) & (key < dead)
             words = empty + total(counted & (group == places), word, 0)
@@ -320,24 +325,29 @@
         skip = HEAD_STEP if j in evens else 0
         theirs = swap(1, block, block, skip)
         return [
-            (block, HEAD, part, both(2 * j)),
-            (theirs, HEAD - skip, part, swapped(j)),
+            (block, HEADS[part], part, both(2 * j)),
+            (theirs, HEADS[part] - skip, part, swapped(j)),
         ]
 
+    def odd_pieces(part):
+        return [piece for j in odds for piece in pieces_of(j, part, odd[part][j])]
+
+    def even_pieces(part):
+        return [piece for j in evens for piece in pieces_of(j, part, even[j][part])]
+
     odd = {}
-    words, lefts = wait(0, words, lefts)
+    wait(0)
     odd[0] = pass_on(0)
-    pieces = [piece for part in parts for piece in pieces_of(0, part, own[part])]
-    pieces += [piece for j in evens for piece in pieces_of(j, 0, even[j][0])]
-    total, left_all = add(None, pieces)
-    odd[0], total = wait(1, odd[0], total)
-    odd[1] = pass_on(1)
-    pieces = [piece for j in odds for piece in pieces_of(j, 0, odd[0][j])]
-    pieces += [piece for j in evens for piece in pieces_of(j, 1, even[j][1])]
-    total = add(total, pieces)
-    odd[1], total = lax.optimization_barrier((odd[1], total))
-    pieces = [piece for j in odds for piece in pieces_of(j, 1, odd[1][j])]
-    return add(total, pieces, closes=True)
+    own_pieces = [pieces_of(0, part, own[part]) for part in parts]
+    pieces = [mine for mine, _ in own_pieces] + [own_pieces[0][1]]
+    total, left_all = add(None, pieces + even_pieces(0))
+    for part in parts[1:]:
+        odd[part - 1], total = wait(part, odd[part - 1], total)
+        odd[part] = pass_on(part)
+        pieces = [own_pieces[part][1]] + odd_pieces(part - 1) + even_pieces(part)
+        total = add(total, pieces)
+    odd[PARTS - 1], total = lax.optimization_barrier((odd[PARTS - 1], total))
+    return add(total, odd_pieces(PARTS - 1), closes=True)
 
 
 def solution(mesh):

time: 57.5 us -> 55.1 us (0.958)
  the two profiles are of different devices: /device:TPU:7 before, /device:TPU:0 now
where the time goes in v2:
time: 55.1 us; the launch traced here: 54.9 us
  Pallas kernels  19.9 us (36%)
  waiting for transfers between devices  17.2 us (31%)
  starting transfers between devices  14.6 us (26%)
  local copies, waits for them, and re-layouts  2.84 us (5%)
    pallas_call x6, Pallas kernels, kernel_call(): pl.pallas_call(kernel, out_shape=out_shape, grid_spec=pltpu.PrefetchScala...  19.9 us
    ppermute x12, waiting for transfers between devices, swap(): return lax.ppermute(mine, 'row', [(i ^ bit, i) for i in range(n_row)])  10.2 us
    ppermute x5, starting transfers between devices, from_ahead(): lax.ppermute(block, axis, [((i + distance) % size, i) for i in range(size)])  9.81 us
    ppermute x5, waiting for transfers between devices, from_ahead(): lax.ppermute(block, axis, [((i + distance) % size, i) for i in range(size)])  7.03 us
    ppermute x12, starting transfers between devices, swap(): return lax.ppermute(mine, 'row', [(i ^ bit, i) for i in range(n_row)])  4.75 us
    unnamed x12, local copies, waits for them, and re-layouts  1.94 us
  transfers between devices with their start and end apart: 17, of which 8 were waited for; matrix products, arithmetic and copies ran while one was open for 2% of the time, Pallas kernels for 29%

profile of v2, /device:TPU:0, one launch (start us, length us, event | category | flops | bytes accessed | tf_op | source)
XLA Modules:
  0.0 54.9 jit_solution(13021424378677273196)
XLA Ops:
  0.0 1.3 %copy-done = bf16[1,1,32,128,128]{4,3,2,1,0:T(8,128)(2,1)S(1)} copy-done((bf16[1,1,32,128,128]{4,3,2,1,0:T(8,128)(2,1)S(1)}, bf16[1,1,32,128,128]{4,3,2,1,0:T(8,128)(2,1)}, u32[]{:S(2)}) %copy-start) | copy-done | bytes 1048600
  1.3 0.7 %copy-done.2 = s32[1,1,32]{2,1,0:T(1,128)S(1)} copy-done((s32[1,1,32]{2,1,0:T(1,128)S(1)}, s32[1,1,32]{2,1,0:T(1,128)}, u32[]{:S(2)}) %copy-start.2) | copy-done | bytes 152
  1.9 0.4 shard_map.74
  2.4 5.1 %collective-permute-start.3 = (bf16[1312,128]{1,0:T(8,128)(2,1)S(1)}, bf16[1312,128]{1,0:T(8,128)(2,1)S(1)}, u32[]{:S(2)}, u32[]{:S(2)}) collective-permute-start(bf16[1312,128]{1,0:T(8,128)(2,1)S(1)} %get-tuple-element.18.refs_2_), channel_id=1, source_target_pairs={{8,0},{10,2},{12,4},{14,6},{16,8},{18,10},{20,12},{22,14},{24,16},... | collective-permute-start | bytes 1007624 | tf_op jit(solution)/shard_map/ppermute | solution.py:258
  7.5 0.0 collective-permute-start.2
  7.5 1.5 %collective-permute-start = (s32[1,16]{1,0:T(1,128)}, s32[1,16]{1,0:T(1,128)S(1)}, u32[]{:S(2)}, u32[]{:S(2)}) collective-permute-start(s32[1,16]{1,0:T(1,128)} %bitcast.12), channel_id=1, source_target_pairs={{1,0},{0,1},{3,2},{2,3},{5,4},{4,5},{7,6},{6,7},{9,8},{8,9},{11,10... | collective-permute-start | bytes 200 | tf_op jit(solution)/shard_map/ppermute | solution.py:258
  9.0 0.5 collective-permute-start.1
  9.5 0.4 collective-permute-start.6
  9.9 0.7 %reshape.19 = s32[8,256]{1,0:T(8,128)S(1)} reshape(s32[1,1,4,2,256]{4,3,2,1,0:T(2,128)} %param.11) | data formatting | bytes 16384 | tf_op jit(solution)/shard_map/reshape | solution.py:280
  10.7 0.1 copy.9
  10.8 5.0 %collective-permute-done.3.refs_6_ = bf16[1312,128]{1,0:T(8,128)(2,1)S(1)} collective-permute-done((bf16[1312,128]{1,0:T(8,128)(2,1)S(1)}, bf16[1312,128]{1,0:T(8,128)(2,1)S(1)}, u32[]{:S(2)}, u32[]{:S(2)}) %collective-permute-start.3) | collective-permute-done | bytes 335904 | tf_op jit(solution)/shard_map/ppermute | solution.py:258
  15.8 0.1 broadcast_select_fusion.2
  15.8 1.6 %collective-permute-start.7 = (bf16[1312,128]{1,0:T(8,128)(2,1)S(1)}, bf16[1312,128]{1,0:T(8,128)(2,1)S(1)}, u32[]{:S(2)}, u32[]{:S(2)}) collective-permute-start(bf16[1312,128]{1,0:T(8,128)(2,1)S(1)} %broadcast_select_fusion.2), channel_id=1, source_target_pairs={{4,0},{6,2},{0,4},{2,6},{12,8},{14,10},{8,12},{10,14},{20,16},{22,... | collective-permute-start | bytes 1007624 | tf_op jit(solution)/shard_map/ppermute | solution.py:263
  17.4 0.0 collective-permute-done.refs_1_
  17.4 0.0 collective-permute-start.4
  17.4 0.0 copy-done.5
  17.4 0.0 copy-start.1
  17.4 3.2 %shard_map.73.words_ref = s32[12,256]{1,0:T(8,128)S(1)} custom-call(s32[1,4]{1,0:T(1,128)S(1)} %bitcast.11, s32[1,4]{1,0:T(1,128)S(1)} %copy-done.4, s32[256,8]{1,0:T(8,128)S(1)} %bitcast.9, s32[1,16]{1,0:T(1,128)S(1)} %bitcast.13, s32[1,16]{1,0:T(1,128)S(1)} %collective-permute-done.refs_1_), custom_call_target="tpu_custom_call" | custom-call | flops 17179869184 | bytes 128 | tf_op jit(solution)/shard_map/pallas_call | solution.py:48
  20.6 0.0 collective-permute-done.2.refs_5_
  20.7 0.6 %collective-permute-start.9 = (bf16[1440,128]{1,0:T(8,128)(2,1)S(1)}, bf16[1440,128]{1,0:T(8,128)(2,1)S(1)}, u32[]{:S(2)}, u32[]{:S(2)}) collective-permute-start(bf16[1440,128]{1,0:T(8,128)(2,1)S(1)} %get-tuple-element.19.refs_3_), channel_id=1, source_target_pairs={{2,0},{0,2},{6,4},{4,6},{10,8},{8,10},{14,12},{12,14},{18,16},{16,... | collective-permute-start | bytes 1105928 | tf_op jit(solution)/shard_map/ppermute | solution.py:263
  21.2 2.0 %collective-permute-done.1.refs_1_ = bf16[2048,128]{1,0:T(8,128)(2,1)S(1)} collective-permute-done((bf16[2048,128]{1,0:T(8,128)(2,1)}, bf16[2048,128]{1,0:T(8,128)(2,1)S(1)}, u32[]{:S(2)}, u32[]{:S(2)}) %collective-permute-start.1) | collective-permute-done | bytes 524320 | tf_op jit(solution)/shard_map/ppermute | solution.py:258
  23.3 2.2 %collective-permute-start.5 = (bf16[1456,128]{1,0:T(8,128)(2,1)S(1)}, bf16[1456,128]{1,0:T(8,128)(2,1)S(1)}, u32[]{:S(2)}, u32[]{:S(2)}) collective-permute-start(bf16[1456,128]{1,0:T(8,128)(2,1)S(1)} %get-tuple-element.20.refs_4_), channel_id=1, source_target_pairs={{8,0},{10,2},{12,4},{14,6},{16,8},{18,10},{20,12},{22,14},{24,16},... | collective-permute-start | bytes 1118216 | tf_op jit(solution)/shard_map/ppermute | solution.py:258
  25.5 0.0 collective-permute-done.4.refs_7_
  25.5 4.4 %shard_map.75 = (f32[32,128,128]{2,1,0:T(8,128)S(1)}, bf16[4224,128]{1,0:T(8,128)(2,1)S(1)}) custom-call(s32[12,256]{1,0:T(8,128)S(1)} %shard_map.73.words_ref, bf16[2048,128]{1,0:T(8,128)(2,1)S(1)} %bitcast.8, bf16[2048,128]{1,0:T(8,128)(2,1)S(1)} %collective-permute-done.1.refs_1_, bf16[1312,128]{1,0:T(8,128)(2,1)S(1)} %get-tuple-element.18.refs_2_, ...), custom_call_target="tpu_custom_call" | custom-call | flops 128 | bytes 128 | tf_op jit(solution)/shard_map/pallas_call | solution.py:48
  29.9 0.0 collective-permute-done.6.refs_4_
  29.9 0.0 collective-permute-done.7.refs_2_
  30.0 0.1 broadcast_select_fusion.1
  30.0 0.1 collective-permute-start.8
  30.1 0.1 collective-permute-start.11
  30.2 0.5 collective-permute-start.10
  30.7 0.0 collective-permute-done.9.refs_1_
  30.7 0.1 collective-permute-start.13
  30.8 1.6 %collective-permute-done.10.refs_3_ = bf16[1312,128]{1,0:T(8,128)(2,1)S(1)} collective-permute-done((bf16[1312,128]{1,0:T(8,128)(2,1)S(1)}, bf16[1312,128]{1,0:T(8,128)(2,1)S(1)}, u32[]{:S(2)}, u32[]{:S(2)}) %collective-permute-start.10) | collective-permute-done | bytes 335904 | tf_op jit(solution)/shard_map/ppermute | solution.py:263
  32.4 0.0 collective-permute-done.11.refs_5_
  32.4 4.1 %shard_map.76.refs_6_ = f32[32,128,128]{2,1,0:T(8,128)S(1)} custom-call(s32[12,256]{1,0:T(8,128)S(1)} %shard_map.73.words_ref, bf16[4224,128]{1,0:T(8,128)(2,1)S(1)} %get-tuple-element.21.refs_0_, bf16[1440,128]{1,0:T(8,128)(2,1)S(1)} %collective-permute-done.9.refs_1_, bf16[1312,128]{1,0:T(8,128)(2,1)S(1)} %collective-permute-done.7.refs_2_, ...), custom_call_target="tpu_custom_call" | custom-call | flops 128 | bytes 128 | tf_op jit(solution)/shard_map/pallas_call | solution.py:48
  36.5 0.0 collective-permute-done.5.refs_4_
  36.5 3.1 %collective-permute-done.8.refs_2_ = bf16[1440,128]{1,0:T(8,128)(2,1)S(1)} collective-permute-done((bf16[1440,128]{1,0:T(8,128)(2,1)S(1)}, bf16[1440,128]{1,0:T(8,128)(2,1)S(1)}, u32[]{:S(2)}, u32[]{:S(2)}) %collective-permute-start.8) | collective-permute-done | bytes 368672 | tf_op jit(solution)/shard_map/ppermute | solution.py:263
  39.7 1.3 %collective-permute-start.12 = (bf16[1456,128]{1,0:T(8,128)(2,1)S(1)}, bf16[1456,128]{1,0:T(8,128)(2,1)S(1)}, u32[]{:S(2)}, u32[]{:S(2)}) collective-permute-start(bf16[1456,128]{1,0:T(8,128)(2,1)S(1)} %broadcast_select_fusion), channel_id=1, source_target_pairs={{4,0},{6,2},{0,4},{2,6},{12,8},{14,10},{8,12},{10,14},{20,16},{22,... | collective-permute-start | bytes 1118216 | tf_op jit(solution)/shard_map/ppermute | solution.py:263
  41.0 0.1 collective-permute-start.15
  41.1 0.5 collective-permute-start.14
  41.6 0.0 collective-permute-done.13.refs_1_
  41.6 1.2 %collective-permute-done.15.refs_5_ = bf16[1440,128]{1,0:T(8,128)(2,1)S(1)} collective-permute-done((bf16[1440,128]{1,0:T(8,128)(2,1)S(1)}, bf16[1440,128]{1,0:T(8,128)(2,1)S(1)}, u32[]{:S(2)}, u32[]{:S(2)}) %collective-permute-start.15) | collective-permute-done | bytes 368672 | tf_op jit(solution)/shard_map/ppermute | solution.py:263
  42.8 0.5 collective-permute-done.14.refs_3_
  43.3 4.0 %shard_map.77.refs_3_ = f32[32,128,128]{2,1,0:T(8,128)S(1)} custom-call(s32[12,256]{1,0:T(8,128)S(1)} %shard_map.73.words_ref, bf16[4224,128]{1,0:T(8,128)(2,1)S(1)} %get-tuple-element.21.refs_0_, bf16[1456,128]{1,0:T(8,128)(2,1)S(1)} %collective-permute-done.13.refs_1_, bf16[1440,128]{1,0:T(8,128)(2,1)S(1)} %collective-permute-done.8.refs_2_, ...), custom_call_target="tpu_custom_call" | custom-call | flops 128 | bytes 128 | tf_op jit(solution)/shard_map/pallas_call | solution.py:48
  47.3 2.1 %collective-permute-done.12.refs_1_ = bf16[1456,128]{1,0:T(8,128)(2,1)S(1)} collective-permute-done((bf16[1456,128]{1,0:T(8,128)(2,1)S(1)}, bf16[1456,128]{1,0:T(8,128)(2,1)S(1)}, u32[]{:S(2)}, u32[]{:S(2)}) %collective-permute-start.12) | collective-permute-done | bytes 372768 | tf_op jit(solution)/shard_map/ppermute | solution.py:263
  49.4 0.0 collective-permute-start.16
  49.4 1.7 %collective-permute-done.16.refs_2_ = bf16[1456,128]{1,0:T(8,128)(2,1)S(1)} collective-permute-done((bf16[1456,128]{1,0:T(8,128)(2,1)S(1)}, bf16[1456,128]{1,0:T(8,128)(2,1)S(1)}, u32[]{:S(2)}, u32[]{:S(2)}) %collective-permute-start.16) | collective-permute-done | bytes 372768 | tf_op jit(solution)/shard_map/ppermute | solution.py:263
  51.0 3.7 %shard_map.78 = bf16[512,1024]{1,0:T(8,128)(2,1)} custom-call(s32[12,256]{1,0:T(8,128)S(1)} %shard_map.73.words_ref, bf16[4224,128]{1,0:T(8,128)(2,1)S(1)} %get-tuple-element.21.refs_0_, bf16[1456,128]{1,0:T(8,128)(2,1)S(1)} %collective-permute-done.12.refs_1_, bf16[1456,128]{1,0:T(8,128)(2,1)S(1)} %collective-permute-done.16.refs_2_, ...), custom_call_target="tpu_custom_call" | custom-call | flops 128 | bytes 128 | tf_op jit(solution)/shard_map/pallas_call | solution.py:48
  (12 shorter events, 0.1 us)
Async XLA Ops:
  0.0 17.4 %copy-start.5 = (s32[1,1,16]{2,1,0:T(1,128)S(1)}, s32[1,1,16]{2,1,0:T(1,128)}, u32[]{:S(2)}) copy-start(s32[1,1,16]{2,1,0:T(1,128)} %param.8) | copy-start | bytes 196
  0.0 17.4 %copy-start.3 = (s32[1,1,4]{2,1,0:T(1,128)S(1)}, s32[1,1,4]{2,1,0:T(1,128)}, u32[]{:S(2)}) copy-start(s32[1,1,4]{2,1,0:T(1,128)} %param.12) | copy-start | bytes 52
  0.0 17.4 %copy-start.4 = (s32[1,4]{1,0:T(1,128)S(1)}, s32[1,4]{1,0:T(1,128)}, u32[]{:S(2)}) copy-start(s32[1,4]{1,0:T(1,128)} %order_ref.1) | copy-start | bytes 52
  0.0 1.3 %copy-start = (bf16[1,1,32,128,128]{4,3,2,1,0:T(8,128)(2,1)S(1)}, bf16[1,1,32,128,128]{4,3,2,1,0:T(8,128)(2,1)}, u32[]{:S(2)}) copy-start(bf16[1,1,32,128,128]{4,3,2,1,0:T(8,128)(2,1)} %param.9) | copy-start | bytes 3145732
  1.3 0.7 %copy-start.2 = (s32[1,1,32]{2,1,0:T(1,128)S(1)}, s32[1,1,32]{2,1,0:T(1,128)}, u32[]{:S(2)}) copy-start(s32[1,1,32]{2,1,0:T(1,128)} %param.10) | copy-start | bytes 388
  2.4 13.4 %collective-permute-start.3 = (bf16[1312,128]{1,0:T(8,128)(2,1)S(1)}, bf16[1312,128]{1,0:T(8,128)(2,1)S(1)}, u32[]{:S(2)}, u32[]{:S(2)}) collective-permute-start(bf16[1312,128]{1,0:T(8,128)(2,1)S(1)} %get-tuple-element.18.refs_2_), channel_id=1, source_target_pairs={{8,0},{10,2},{12,4},{14,6},{16,8},{18,10},{20,12},{22,14},{24,16},... | collective-permute-start | bytes 1007624 | tf_op jit(solution)/shard_map/ppermute | solution.py:258
  7.5 13.2 %collective-permute-start.2 = (bf16[1312,128]{1,0:T(8,128)(2,1)S(1)}, bf16[1312,128]{1,0:T(8,128)(2,1)S(1)}, u32[]{:S(2)}, u32[]{:S(2)}) collective-permute-start(bf16[1312,128]{1,0:T(8,128)(2,1)S(1)} %get-tuple-element.18.refs_2_), channel_id=1, source_target_pairs={{2,0},{0,2},{6,4},{4,6},{10,8},{8,10},{14,12},{12,14},{18,16},{16,... | collective-permute-start | bytes 1007624 | tf_op jit(solution)/shard_map/ppermute | solution.py:263
  7.5 9.9 %collective-permute-start = (s32[1,16]{1,0:T(1,128)}, s32[1,16]{1,0:T(1,128)S(1)}, u32[]{:S(2)}, u32[]{:S(2)}) collective-permute-start(s32[1,16]{1,0:T(1,128)} %bitcast.12), channel_id=1, source_target_pairs={{1,0},{0,1},{3,2},{2,3},{5,4},{4,5},{7,6},{6,7},{9,8},{8,9},{11,10... | collective-permute-start | bytes 200 | tf_op jit(solution)/shard_map/ppermute | solution.py:258
  9.0 14.3 %collective-permute-start.1 = (bf16[2048,128]{1,0:T(8,128)(2,1)}, bf16[2048,128]{1,0:T(8,128)(2,1)S(1)}, u32[]{:S(2)}, u32[]{:S(2)}) collective-permute-start(bf16[2048,128]{1,0:T(8,128)(2,1)} %bitcast.7), channel_id=1, source_target_pairs={{1,0},{0,1},{3,2},{2,3},{5,4},{4,5},{7,6},{6,7},{9,8},{8,9},{11,10... | collective-permute-start | bytes 1572872 | tf_op jit(solution)/shard_map/ppermute | solution.py:258
  9.5 20.4 %collective-permute-start.6 = (bf16[1440,128]{1,0:T(8,128)(2,1)S(1)}, bf16[1440,128]{1,0:T(8,128)(2,1)S(1)}, u32[]{:S(2)}, u32[]{:S(2)}) collective-permute-start(bf16[1440,128]{1,0:T(8,128)(2,1)S(1)} %get-tuple-element.19.refs_3_), channel_id=1, source_target_pairs={{8,0},{10,2},{12,4},{14,6},{16,8},{18,10},{20,12},{22,14},{24,16},... | collective-permute-start | bytes 1105928 | tf_op jit(solution)/shard_map/ppermute | solution.py:258
  15.8 14.1 %collective-permute-start.7 = (bf16[1312,128]{1,0:T(8,128)(2,1)S(1)}, bf16[1312,128]{1,0:T(8,128)(2,1)S(1)}, u32[]{:S(2)}, u32[]{:S(2)}) collective-permute-start(bf16[1312,128]{1,0:T(8,128)(2,1)S(1)} %broadcast_select_fusion.2), channel_id=1, source_target_pairs={{4,0},{6,2},{0,4},{2,6},{12,8},{14,10},{8,12},{10,14},{20,16},{22,... | collective-permute-start | bytes 1007624 | tf_op jit(solution)/shard_map/ppermute | solution.py:263
  17.4 8.1 %collective-permute-start.4 = (bf16[1296,128]{1,0:T(8,128)(2,1)S(1)}, bf16[1296,128]{1,0:T(8,128)(2,1)S(1)}, u32[]{:S(2)}, u32[]{:S(2)}) collective-permute-start(bf16[1296,128]{1,0:T(8,128)(2,1)S(1)} %slice.12), channel_id=1, source_target_pairs={{2,0},{0,2},{6,4},{4,6},{10,8},{8,10},{14,12},{12,14},{18,16},{16,... | collective-permute-start | bytes 995336 | tf_op jit(solution)/shard_map/ppermute | solution.py:263
  17.4 8.1 %copy-start.1 = (bf16[1,1,16,128,128]{4,3,2,1,0:T(8,128)(2,1)S(1)}, bf16[1,1,16,128,128]{4,3,2,1,0:T(8,128)(2,1)}, u32[]{:S(2)}) copy-start(bf16[1,1,16,128,128]{4,3,2,1,0:T(8,128)(2,1)} %param.7) | copy-start | bytes 1572868
  20.7 10.1 %collective-permute-start.9 = (bf16[1440,128]{1,0:T(8,128)(2,1)S(1)}, bf16[1440,128]{1,0:T(8,128)(2,1)S(1)}, u32[]{:S(2)}, u32[]{:S(2)}) collective-permute-start(bf16[1440,128]{1,0:T(8,128)(2,1)S(1)} %get-tuple-element.19.refs_3_), channel_id=1, source_target_pairs={{2,0},{0,2},{6,4},{4,6},{10,8},{8,10},{14,12},{12,14},{18,16},{16,... | collective-permute-start | bytes 1105928 | tf_op jit(solution)/shard_map/ppermute | solution.py:263
  23.3 13.2 %collective-permute-start.5 = (bf16[1456,128]{1,0:T(8,128)(2,1)S(1)}, bf16[1456,128]{1,0:T(8,128)(2,1)S(1)}, u32[]{:S(2)}, u32[]{:S(2)}) collective-permute-start(bf16[1456,128]{1,0:T(8,128)(2,1)S(1)} %get-tuple-element.20.refs_4_), channel_id=1, source_target_pairs={{8,0},{10,2},{12,4},{14,6},{16,8},{18,10},{20,12},{22,14},{24,16},... | collective-permute-start | bytes 1118216 | tf_op jit(solution)/shard_map/ppermute | solution.py:258
  30.0 9.6 %collective-permute-start.8 = (bf16[1440,128]{1,0:T(8,128)(2,1)S(1)}, bf16[1440,128]{1,0:T(8,128)(2,1)S(1)}, u32[]{:S(2)}, u32[]{:S(2)}) collective-permute-start(bf16[1440,128]{1,0:T(8,128)(2,1)S(1)} %broadcast_select_fusion.1), channel_id=1, source_target_pairs={{4,0},{6,2},{0,4},{2,6},{12,8},{14,10},{8,12},{10,14},{20,16},{22,... | collective-permute-start | bytes 1105928 | tf_op jit(solution)/shard_map/ppermute | solution.py:263
  30.1 2.2 %collective-permute-start.11 = (bf16[1424,128]{1,0:T(8,128)(2,1)S(1)}, bf16[1424,128]{1,0:T(8,128)(2,1)S(1)}, u32[]{:S(2)}, u32[]{:S(2)}) collective-permute-start(bf16[1424,128]{1,0:T(8,128)(2,1)S(1)} %slice.10), channel_id=1, source_target_pairs={{2,0},{0,2},{6,4},{4,6},{10,8},{8,10},{14,12},{12,14},{18,16},{16,... | collective-permute-start | bytes 1093640 | tf_op jit(solution)/shard_map/ppermute | solution.py:263
  30.2 2.1 %collective-permute-start.10 = (bf16[1312,128]{1,0:T(8,128)(2,1)S(1)}, bf16[1312,128]{1,0:T(8,128)(2,1)S(1)}, u32[]{:S(2)}, u32[]{:S(2)}) collective-permute-start(bf16[1312,128]{1,0:T(8,128)(2,1)S(1)} %collective-permute-done.7.refs_2_), channel_id=1, source_target_pairs={{2,0},{0,2},{6,4},{4,6},{10,8},{8,10},{14,12},{12,14},{18,16},{16,... | collective-permute-start | bytes 1007624 | tf_op jit(solution)/shard_map/ppermute | solution.py:263
  30.7 10.9 %collective-permute-start.13 = (bf16[1456,128]{1,0:T(8,128)(2,1)S(1)}, bf16[1456,128]{1,0:T(8,128)(2,1)S(1)}, u32[]{:S(2)}, u32[]{:S(2)}) collective-permute-start(bf16[1456,128]{1,0:T(8,128)(2,1)S(1)} %get-tuple-element.20.refs_4_), channel_id=1, source_target_pairs={{2,0},{0,2},{6,4},{4,6},{10,8},{8,10},{14,12},{12,14},{18,16},{16,... | collective-permute-start | bytes 1118216 | tf_op jit(solution)/shard_map/ppermute | solution.py:263
  39.7 9.7 %collective-permute-start.12 = (bf16[1456,128]{1,0:T(8,128)(2,1)S(1)}, bf16[1456,128]{1,0:T(8,128)(2,1)S(1)}, u32[]{:S(2)}, u32[]{:S(2)}) collective-permute-start(bf16[1456,128]{1,0:T(8,128)(2,1)S(1)} %broadcast_select_fusion), channel_id=1, source_target_pairs={{4,0},{6,2},{0,4},{2,6},{12,8},{14,10},{8,12},{10,14},{20,16},{22,... | collective-permute-start | bytes 1118216 | tf_op jit(solution)/shard_map/ppermute | solution.py:263
  41.0 1.8 %collective-permute-start.15 = (bf16[1440,128]{1,0:T(8,128)(2,1)S(1)}, bf16[1440,128]{1,0:T(8,128)(2,1)S(1)}, u32[]{:S(2)}, u32[]{:S(2)}) collective-permute-start(bf16[1440,128]{1,0:T(8,128)(2,1)S(1)} %slice.11), channel_id=1, source_target_pairs={{2,0},{0,2},{6,4},{4,6},{10,8},{8,10},{14,12},{12,14},{18,16},{16,... | collective-permute-start | bytes 1105928 | tf_op jit(solution)/shard_map/ppermute | solution.py:263
  41.1 2.2 %collective-permute-start.14 = (bf16[1440,128]{1,0:T(8,128)(2,1)S(1)}, bf16[1440,128]{1,0:T(8,128)(2,1)S(1)}, u32[]{:S(2)}, u32[]{:S(2)}) collective-permute-start(bf16[1440,128]{1,0:T(8,128)(2,1)S(1)} %collective-permute-done.8.refs_2_), channel_id=1, source_target_pairs={{2,0},{0,2},{6,4},{4,6},{10,8},{8,10},{14,12},{12,14},{18,16},{16,... | collective-permute-start | bytes 1105928 | tf_op jit(solution)/shard_map/ppermute | solution.py:263
  49.4 1.7 %collective-permute-start.16 = (bf16[1456,128]{1,0:T(8,128)(2,1)S(1)}, bf16[1456,128]{1,0:T(8,128)(2,1)S(1)}, u32[]{:S(2)}, u32[]{:S(2)}) collective-permute-start(bf16[1456,128]{1,0:T(8,128)(2,1)S(1)} %collective-permute-done.12.refs_1_), channel_id=1, source_target_pairs={{2,0},{0,2},{6,4},{4,6},{10,8},{8,10},{14,12},{12,14},{18,16},{16,... | collective-permute-start | bytes 1118216 | tf_op jit(solution)/shard_map/ppermute | solution.py:263
